TPU v7x, 32 devices: a whole 2x2x4 slice. The times are simulated.
32 devices in a mesh: seq: 4 (over y, core), exp: 8 (over z, x).
Axes of the slice: x: 2, y: 2, z: 4, core: 2. Of those that a mesh axis runs over, the one named last changes fastest.
Arguments:
- frames: bfloat16 [8, 512, 1024], P('exp', 'seq'), may hold values from -6 to 6
- conv_kernel: float32 [31, 1024], replicated, may hold values from -1 to 1
- routes: int32 [8, 512, 2], P('exp', 'seq'), may hold values from 0 to 31, all different within a row; in each aligned block of 128 rows (0 to 127, 128 to 255, ..., all dimensions but the last counted through in order) at most 8 rows name the same one
- gates: float32 [8, 512, 2], P('exp', 'seq'), may hold values from 0.25 to 1
- w_in: bfloat16 [32, 1024, 2048], P('exp', None, 'seq'), may hold values from -0.1875 to 0.1875
- w_out: bfloat16 [32, 2048, 1024], P('exp', 'seq'), may hold values from -0.125 to 0.125
- cotangent: bfloat16 [8, 512, 1024], P('exp', 'seq'), may hold values from -1.5 to 1.5
Outputs:
- mixed: bfloat16 [8, 512, 1024], P('exp', 'seq')
- frames_grad: bfloat16 [8, 512, 1024], P('exp', 'seq')
- w_in_grad: float32 [32, 1024, 2048], P('exp', None, 'seq')
- w_out_grad: float32 [32, 2048, 1024], P('exp', 'seq')
Inputs may be any that keep to these rules, and one draw needn't show every extreme that they name: `routes`: each frame names two different experts. Within each aligned block of 128 frames of a recording no expert is named more than 8 times, and in every draw some expert is named exactly 8 times within some block.
All inputs are finite; a program needn't handle non-finite values.
Results may differ from a plain program's by a relative error of at most 0.012.
Values may be sent and summed in bfloat16 or wider, within the bound.
A program may use at most 192 MiB of HBM per device.

v0:
```python
import jax
import jax.numpy as jnp
from jax import lax
from jax.sharding import PartitionSpec as P

KERNEL = 31
CAP = 8


def extended(block, sides, width):
    for axis, dim in sides:
        count = lax.axis_size(axis)
        forward = [(i, i + 1) for i in range(count - 1)]
        backward = [(target, source) for source, target in forward]
        low = lax.ppermute(
            lax.slice_in_dim(block, block.shape[dim] - width, None, axis=dim), axis, forward
        )
        high = lax.ppermute(lax.slice_in_dim(block, 0, width, axis=dim), axis, backward)
        block = jnp.concatenate([low, block, high], axis=dim)
    return block


def silu_slope(values):
    logistic = jax.nn.sigmoid(values)
    return logistic * (1.0 + values * (1.0 - logistic))


def edge_rows(field):
    return extended(field, (("seq", 1),), (KERNEL - 1) // 2)


def local_conv(padded, kernel, reverse, length):
    margin = (KERNEL - 1) // 2
    summed = jnp.zeros((padded.shape[0], length, padded.shape[2]), jnp.float32)
    for tap_index in range(KERNEL):
        offset = 2 * margin - tap_index if reverse else tap_index
        summed = summed + kernel[tap_index] * padded[:, offset : offset + length, :]
    return summed


def to_sources(term_fn, groups, n_seq, n_exp, per_dest, model_width):
    whole_term = term_fn(0, groups).astype(jnp.bfloat16).reshape(groups, per_dest, model_width)
    arrived = lax.all_to_all(whole_term, ("seq", "exp"), split_axis=0, concat_axis=0, tiled=True)
    summed = jnp.sum(
        arrived.reshape(n_seq, n_exp, per_dest, model_width).astype(jnp.float32), axis=0
    ).astype(jnp.bfloat16)
    return summed.reshape(n_exp * per_dest, model_width)


def per_device(frames, conv_kernel, routes, gates, w_in, w_out, cotangent):
    n_seq = lax.axis_size("seq")
    n_exp = lax.axis_size("exp")
    local_experts = w_in.shape[0]
    all_experts = local_experts * n_exp
    length = frames.shape[1]
    model_width = frames.shape[2]
    groups = n_seq * n_exp
    per_dest = local_experts * CAP
    mixing = local_conv(edge_rows(frames).astype(jnp.float32), conv_kernel, False, length)
    hidden = (frames.astype(jnp.float32) + jax.nn.silu(mixing)).astype(jnp.bfloat16)
    flat_hidden = hidden[0]
    expert_ids = routes[0].reshape(2 * length)
    onehot = (expert_ids[:, None] == jnp.arange(all_experts, dtype=jnp.int32)[None, :]).astype(
        jnp.int32
    )
    slot_rank = jnp.sum((jnp.cumsum(onehot, axis=0) - onehot) * onehot, axis=1)
    places = expert_ids * CAP + slot_rank
    gate_pair = gates[0]
    up_rows = jnp.repeat(flat_hidden, 2, axis=0)
    down_rows = (
        gate_pair.reshape(2 * length, 1) * jnp.repeat(cotangent[0].astype(jnp.float32), 2, axis=0)
    ).astype(jnp.bfloat16)
    blank_slots = jnp.zeros((all_experts * CAP, model_width), jnp.bfloat16)
    send_up = blank_slots.at[places].set(up_rows).reshape(n_exp, per_dest, model_width)
    send_down = blank_slots.at[places].set(down_rows).reshape(n_exp, per_dest, model_width)
    wide_up = jnp.broadcast_to(send_up[None], (n_seq, n_exp, per_dest, model_width)).reshape(
        groups, per_dest, model_width
    )
    wide_down = jnp.broadcast_to(send_down[None], (n_seq, n_exp, per_dest, model_width)).reshape(
        groups, per_dest, model_width
    )
    got_up, got_down = (
        lax.all_to_all(wide_up, ("seq", "exp"), split_axis=0, concat_axis=0, tiled=True),
        lax.all_to_all(wide_down, ("seq", "exp"), split_axis=0, concat_axis=0, tiled=True),
    )
    routed_up = got_up.reshape(groups, local_experts, CAP, model_width)
    routed_down = got_down.reshape(groups, local_experts, CAP, model_width)
    pre_act = jnp.einsum("gecd,edh->gech", routed_up, w_in, preferred_element_type=jnp.float32)
    activation = jax.nn.silu(pre_act).astype(jnp.bfloat16)

    def forward_term(offset, row_count):
        return jnp.einsum("gech,ehd->gecd", activation, w_out, preferred_element_type=jnp.float32)

    expert_out = to_sources(forward_term, groups, n_seq, n_exp, per_dest, model_width)
    picked = expert_out[places].reshape(length, 2, model_width).astype(jnp.float32)
    mixed = (
        flat_hidden.astype(jnp.float32) + jnp.sum(gate_pair[:, :, None] * picked, axis=1)
    ).astype(jnp.bfloat16)
    act_grad = jnp.einsum("gecd,ehd->gech", routed_down, w_out, preferred_element_type=jnp.float32)
    pre_grad = (act_grad * silu_slope(pre_act)).astype(jnp.bfloat16)
    w_out_grad = jnp.einsum(
        "gech,gecd->ehd", activation, routed_down, preferred_element_type=jnp.float32
    )
    w_in_grad = jnp.einsum(
        "gecd,gech->edh", routed_up, pre_grad, preferred_element_type=jnp.float32
    )

    def backward_term(offset, row_count):
        return jnp.einsum("gech,edh->gecd", pre_grad, w_in, preferred_element_type=jnp.float32)

    input_grad = to_sources(backward_term, groups, n_seq, n_exp, per_dest, model_width)
    back_rows = input_grad[places].reshape(length, 2, model_width).astype(jnp.float32)
    hidden_grad = cotangent[0].astype(jnp.float32) + jnp.sum(back_rows, axis=1)
    conv_back = (hidden_grad * silu_slope(mixing[0])).astype(jnp.bfloat16)
    spread = local_conv(edge_rows(conv_back[None]).astype(jnp.float32), conv_kernel, True, length)
    frames_grad = (hidden_grad + spread[0]).astype(jnp.bfloat16)
    return (mixed[None], frames_grad[None], w_in_grad, w_out_grad)


def solution(mesh):
    in_specs = (
        P("exp", "seq", None),
        P(),
        P("exp", "seq", None),
        P("exp", "seq", None),
        P("exp", None, "seq"),
        P("exp", "seq", None),
        P("exp", "seq", None),
    )
    out_specs = (
        P("exp", "seq", None),
        P("exp", "seq", None),
        P("exp", None, "seq"),
        P("exp", "seq", None),
    )
    return jax.shard_map(
        per_device, mesh=mesh, in_specs=in_specs, out_specs=out_specs, check_vma=False
    )
```

profile of v0, /device:TPU:1, one launch (start us, length us, event | category | flops | bytes accessed | tf_op | source)
XLA Modules:
  0.0 259.0 jit_solution(6836123576873928668)
XLA Ops:
  0.6 0.8 fusion.104
  1.5 4.5 %collective-permute-start = (bf16[1,15,1024]{2,1,0:T(8,128)(2,1)S(1)}, bf16[1,15,1024]{2,1,0:T(8,128)(2,1)S(1)}, u32[]{:S(2)}, u32[]{:S(2)}) collective-permute-start(bf16[1,15,1024]{2,1,0:T(8,128)(2,1)S(1)} %get-tuple-element.8), channel_id=1, source_target_pairs={{0,8},{8,16},{16,24},{1,9},{9,17},{17,25},{2,10},{10,18},{18,26},{... | collective-permute-start | bytes 92168 | tf_op jit(solution)/shard_map/ppermute | solution.py:15
  6.0 1.9 collective-permute-start.1
  8.0 0.7 broadcast_multiply_fusion
  8.6 0.8 copy.18
  9.7 1.1 fusion.106
  10.8 1.4 fusion.105
  13.6 1.0 maximum_convert_fusion
  14.7 2.9 %add_convert_fusion = (bf16[1,128,1024]{2,1,0:T(8,128)(2,1)S(1)}, f32[1,128,1024]{2,1,0:T(8,128)}) fusion(bf16[1,128,1024]{2,1,0:T(8,128)(2,1)S(1)} %copy-done.10, f32[1,158,1024]{2,1,0:T(8,128)S(1)} %maximum_convert_fusion, f32[1024]{0:T(1024)S(1)} %bitcast.181, f32[1024]{0:T(1024)S(1)} %bitcast.183, f32[1024]{0:T(1024)S(1)} %bitcast.187, ...), kind=kLoop, calls=%fused_computation.166 | loop fusion | flops 8912896 | bytes 17428480 | tf_op jit(solution)/shard_map/convert_element_type | solution.py:60
  17.7 0.7 copy-done.4
  18.9 1.8 scatter_custom_fusion
  20.7 1.6 broadcast_in_dim.34
  22.3 6.2 %all-to-all-start = ((bf16[32,32,1024]{2,1,0:T(8,128)(2,1)}), bf16[32,32,1024]{2,1,0:T(8,128)(2,1)S(1)}, u32[]{:S(2)}, u32[]{:S(2)}) async-start(bf16[32,32,1024]{2,1,0:T(8,128)(2,1)} %bitcast.37), calls=%async_computation | async-start | bytes 4194304 | tf_op jit(solution)/shard_map/all_to_all | solution.py:83
  28.8 1.3 broadcast_in_dim.35
  30.1 1.9 reshape.284
  32.1 2.5 scatter_custom_fusion.1
  34.6 43.3 %all-to-all-done = bf16[32,32,1024]{2,1,0:T(8,128)(2,1)S(1)} async-done(((bf16[32,32,1024]{2,1,0:T(8,128)(2,1)}), bf16[32,32,1024]{2,1,0:T(8,128)(2,1)S(1)}, u32[]{:S(2)}, u32[]{:S(2)}) %all-to-all-start) | async-done | bytes 2097184 | tf_op jit(solution)/shard_map/all_to_all | solution.py:83
  78.0 3.0 %broadcast_in_dim.37 = bf16[4,8,32,1024]{3,2,1,0:T(8,128)(2,1)} broadcast(bf16[8,32,1024]{2,1,0:T(8,128)(2,1)} %bitcast.159), dimensions={1,2,3} | broadcast | bytes 2621440 | tf_op jit(solution)/shard_map/broadcast_in_dim | solution.py:79
  80.9 3.9 %all-to-all-start.2 = ((bf16[32,32,1024]{2,1,0:T(8,128)(2,1)}), bf16[32,32,1024]{2,1,0:T(8,128)(2,1)}, u32[]{:S(2)}, u32[]{:S(2)}) async-start(bf16[32,32,1024]{2,1,0:T(8,128)(2,1)} %bitcast.51), calls=%async_computation.2 | async-start | bytes 4194304 | tf_op jit(solution)/shard_map/all_to_all | solution.py:84
  84.9 4.8 %fusion.2 = f32[4,32,8,512]{3,2,1,0:T(8,128)} fusion(bf16[4,1024,512]{2,1,0:T(8,128)(2,1)} %param.11, bf16[32,32,1024]{2,1,0:T(8,128)(2,1)S(1)} %all-to-all-done), kind=kOutput, calls=%fused_computation.6 | convolution fusion | flops 1073741824 | bytes 8388608 | tf_op jit(solution)/shard_map/gecd,edh->gech/dot_general | solution.py:88
  89.6 44.9 %all-to-all-done.2 = bf16[32,32,1024]{2,1,0:T(8,128)(2,1)} async-done(((bf16[32,32,1024]{2,1,0:T(8,128)(2,1)}), bf16[32,32,1024]{2,1,0:T(8,128)(2,1)}, u32[]{:S(2)}, u32[]{:S(2)}) %all-to-all-start.2) | async-done | bytes 2097184 | tf_op jit(solution)/shard_map/all_to_all | solution.py:84
  134.5 5.2 %fusion.8 = bf16[32,4,8,512]{3,2,0,1:T(8,128)(2,1)S(1)} fusion(f32[4,32,8,512]{3,2,1,0:T(8,128)} %fusion.2, bf16[4,512,1024]{2,1,0:T(8,128)(2,1)} %param.12, bf16[32,32,1024]{2,1,0:T(8,128)(2,1)} %all-to-all-done.2), kind=kOutput, calls=%fused_computation.15 | convolution fusion | flops 1078460416 | bytes 9437184 | tf_op jit(solution)/shard_map/gecd,ehd->gech/dot_general | solution.py:99
  139.7 1.3 convert_bitcast_fusion
  141.0 1.5 copy.53
  142.5 3.8 %all-to-all-start.3 = ((bf16[32,32,1024]{2,1,0:T(8,128)(2,1)}), bf16[32,32,1024]{2,1,0:T(8,128)(2,1)S(1)}, u32[]{:S(2)}, u32[]{:S(2)}) async-start(bf16[32,32,1024]{2,1,0:T(8,128)(2,1)} %bitcast.157), calls=%async_computation.3 | async-start | bytes 4194304 | tf_op jit(solution)/shard_map/all_to_all | solution.py:43
  146.4 0.8 copy.16
  147.1 1.3 pad_clamp_fusion
  148.4 4.1 %convert_bitcast_fusion.1 = bf16[32,4,8,1024]{3,2,0,1:T(8,128)(2,1)S(1)} fusion(bf16[4,512,1024]{2,1,0:T(8,128)(2,1)} %param.12, f32[4,32,8,512]{3,2,1,0:T(8,128)} %fusion.2), kind=kOutput, calls=%fused_computation.29 | convolution fusion | flops 1077411840 | bytes 8388608 | tf_op jit(solution)/shard_map/gech,ehd->gecd/dot_general | solution.py:92
  152.5 1.6 copy.54
  154.1 41.7 %all-to-all-done.3 = bf16[32,32,1024]{2,1,0:T(8,128)(2,1)S(1)} async-done(((bf16[32,32,1024]{2,1,0:T(8,128)(2,1)}), bf16[32,32,1024]{2,1,0:T(8,128)(2,1)S(1)}, u32[]{:S(2)}, u32[]{:S(2)}) %all-to-all-start.3) | async-done | bytes 2097184 | tf_op jit(solution)/shard_map/all_to_all | solution.py:43
  195.8 1.4 copy-done.1
  197.2 3.8 %all-to-all-start.1 = ((bf16[32,32,1024]{2,1,0:T(8,128)(2,1)}), bf16[32,32,1024]{2,1,0:T(8,128)(2,1)S(1)}, u32[]{:S(2)}, u32[]{:S(2)}) async-start(bf16[32,32,1024]{2,1,0:T(8,128)(2,1)} %bitcast.150), calls=%async_computation.1 | async-start | bytes 4194304 | tf_op jit(solution)/shard_map/all_to_all | solution.py:43
  201.1 6.4 %convolution_bitcast_fusion.1 = f32[4,1024,512]{2,1,0:T(8,128)} fusion(bf16[32,4,8,512]{3,2,0,1:T(8,128)(2,1)S(1)} %fusion.8, bf16[32,32,1024]{2,1,0:T(8,128)(2,1)} %copy-done.2), kind=kOutput, calls=%fused_computation.13 | convolution fusion | flops 1073741824 | bytes 11534336 | tf_op jit(solution)/shard_map/gecd,gech->edh/dot_general | solution.py:104
  207.5 6.4 %convolution_bitcast_fusion = f32[4,512,1024]{2,1,0:T(8,128)} fusion(f32[4,32,8,512]{3,2,1,0:T(8,128)S(1)} %copy-done.6, bf16[32,32,1024]{2,1,0:T(8,128)(2,1)} %all-to-all-done.2), kind=kOutput, calls=%fused_computation.12 | convolution fusion | flops 1076363264 | bytes 12582912 | tf_op jit(solution)/shard_map/gech,gecd->ehd/dot_general | solution.py:101
  213.9 2.0 reduce_sum.62
  215.9 1.3 gather_fusion.1
  217.2 1.6 reshape.292
  218.9 2.5 reduce_sum.63
  221.6 0.7 fusion.103
  222.3 3.5 %collective-permute-start.2 = (bf16[1,15,1024]{2,1,0:T(8,128)(2,1)}, bf16[1,15,1024]{2,1,0:T(8,128)(2,1)}, u32[]{:S(2)}, u32[]{:S(2)}) collective-permute-start(bf16[1,15,1024]{2,1,0:T(8,128)(2,1)} %get-tuple-element.6), channel_id=1, source_target_pairs={{0,8},{8,16},{16,24},{1,9},{9,17},{17,25},{2,10},{10,18},{18,26},{... | collective-permute-start | bytes 92168 | tf_op jit(solution)/shard_map/ppermute | solution.py:15
  225.8 2.1 collective-permute-start.3
  228.0 22.6 %all-to-all-done.1 = bf16[32,32,1024]{2,1,0:T(8,128)(2,1)S(1)} async-done(((bf16[32,32,1024]{2,1,0:T(8,128)(2,1)}), bf16[32,32,1024]{2,1,0:T(8,128)(2,1)S(1)}, u32[]{:S(2)}, u32[]{:S(2)}) %all-to-all-start.1) | async-done | bytes 2097184 | tf_op jit(solution)/shard_map/all_to_all | solution.py:43
  251.0 1.3 gather_fusion
  252.3 0.7 reshape.290
  253.1 1.3 multiply_reduce_fusion
  254.4 0.8 fusion.90
  255.2 0.9 maximum_convert_fusion.1
  256.2 2.8 %fusion.30 = bf16[1,128,1024]{2,1,0:T(8,128)(2,1)} fusion(f32[1,158,1024]{2,1,0:T(8,128)S(1)} %maximum_convert_fusion.1, f32[128,1024]{1,0:T(8,128)S(1)} %reduce_sum.63, bf16[1,128,1024]{2,1,0:T(8,128)(2,1)S(1)} %copy-done.3, f32[1024]{0:T(1024)S(1)} %bitcast.182, f32[1024]{0:T(1024)S(1)} %bitcast.184, f32[1024]{0:T(1024)S(1)} %bitcast.188, ...), kind=kLoop, calls=%fused_computation.41 | loop fusion | flops 8519680 | bytes 17428480 | tf_op jit(solution)/shard_map/convert_element_type | solution.py:116
  (90 shorter events, 3.0 us)
Async XLA Ops:
  0.6 14.0 %copy-start.10 = (bf16[1,128,1024]{2,1,0:T(8,128)(2,1)S(1)}, bf16[1,128,1024]{2,1,0:T(8,128)(2,1)}, u32[]{:S(2)}) copy-start(bf16[1,128,1024]{2,1,0:T(8,128)(2,1)} %param.7) | copy-start | bytes 786436
  1.5 12.1 %collective-permute-start = (bf16[1,15,1024]{2,1,0:T(8,128)(2,1)S(1)}, bf16[1,15,1024]{2,1,0:T(8,128)(2,1)S(1)}, u32[]{:S(2)}, u32[]{:S(2)}) collective-permute-start(bf16[1,15,1024]{2,1,0:T(8,128)(2,1)S(1)} %get-tuple-element.8), channel_id=1, source_target_pairs={{0,8},{8,16},{16,24},{1,9},{9,17},{17,25},{2,10},{10,18},{18,26},{... | collective-permute-start | bytes 92168 | tf_op jit(solution)/shard_map/ppermute | solution.py:15
  6.0 7.6 %collective-permute-start.1 = (bf16[1,15,1024]{2,1,0:T(8,128)(2,1)S(1)}, bf16[1,15,1024]{2,1,0:T(8,128)(2,1)S(1)}, u32[]{:S(2)}, u32[]{:S(2)}) collective-permute-start(bf16[1,15,1024]{2,1,0:T(8,128)(2,1)S(1)} %get-tuple-element.9), channel_id=1, source_target_pairs={{8,0},{16,8},{24,16},{9,1},{17,9},{25,17},{10,2},{18,10},{26,18},{... | collective-permute-start | bytes 92168 | tf_op jit(solution)/shard_map/ppermute | solution.py:18
  12.3 5.3 %copy-start.11 = (f32[1,1024]{1,0:T(1,128)}, f32[1,1024]{1,0:T(1,128)S(1)}, u32[]{:S(2)}) copy-start(f32[1,1024]{1,0:T(1,128)S(1)} %get-tuple-element.18) | copy-start | bytes 12292
  12.3 5.3 %copy-start.13 = (f32[1,1024]{1,0:T(1,128)}, f32[1,1024]{1,0:T(1,128)S(1)}, u32[]{:S(2)}) copy-start(f32[1,1024]{1,0:T(1,128)S(1)} %get-tuple-element.19) | copy-start | bytes 12292
  12.3 5.3 %copy-start.15 = (f32[1,1024]{1,0:T(1,128)}, f32[1,1024]{1,0:T(1,128)S(1)}, u32[]{:S(2)}) copy-start(f32[1,1024]{1,0:T(1,128)S(1)} %get-tuple-element.20) | copy-start | bytes 12292
  12.3 5.3 %copy-start.17 = (f32[1,1024]{1,0:T(1,128)}, f32[1,1024]{1,0:T(1,128)S(1)}, u32[]{:S(2)}) copy-start(f32[1,1024]{1,0:T(1,128)S(1)} %get-tuple-element.21) | copy-start | bytes 12292
  12.3 5.3 %copy-start.19 = (f32[1,1024]{1,0:T(1,128)}, f32[1,1024]{1,0:T(1,128)S(1)}, u32[]{:S(2)}) copy-start(f32[1,1024]{1,0:T(1,128)S(1)} %get-tuple-element.22) | copy-start | bytes 12292
  12.3 5.3 %copy-start.21 = (f32[1,1024]{1,0:T(1,128)}, f32[1,1024]{1,0:T(1,128)S(1)}, u32[]{:S(2)}) copy-start(f32[1,1024]{1,0:T(1,128)S(1)} %get-tuple-element.23) | copy-start | bytes 12292
  12.3 5.3 %copy-start.23 = (f32[1,1024]{1,0:T(1,128)}, f32[1,1024]{1,0:T(1,128)S(1)}, u32[]{:S(2)}) copy-start(f32[1,1024]{1,0:T(1,128)S(1)} %get-tuple-element.24) | copy-start | bytes 12292
  12.3 5.3 %copy-start.25 = (f32[1,1024]{1,0:T(1,128)}, f32[1,1024]{1,0:T(1,128)S(1)}, u32[]{:S(2)}) copy-start(f32[1,1024]{1,0:T(1,128)S(1)} %get-tuple-element.25) | copy-start | bytes 12292
  12.3 5.3 %copy-start.27 = (f32[1,1024]{1,0:T(1,128)}, f32[1,1024]{1,0:T(1,128)S(1)}, u32[]{:S(2)}) copy-start(f32[1,1024]{1,0:T(1,128)S(1)} %get-tuple-element.26) | copy-start | bytes 12292
  12.3 5.3 %copy-start.29 = (f32[1,1024]{1,0:T(1,128)}, f32[1,1024]{1,0:T(1,128)S(1)}, u32[]{:S(2)}) copy-start(f32[1,1024]{1,0:T(1,128)S(1)} %get-tuple-element.27) | copy-start | bytes 12292
  12.4 5.3 %copy-start.31 = (f32[1,1024]{1,0:T(1,128)}, f32[1,1024]{1,0:T(1,128)S(1)}, u32[]{:S(2)}) copy-start(f32[1,1024]{1,0:T(1,128)S(1)} %get-tuple-element.28) | copy-start | bytes 12292
  13.6 18.5 %copy-start.34 = (s32[256,1]{0,1:T(1,128)}, s32[256,1]{0,1:T(1,128)S(1)}, u32[]{:S(2)}) copy-start(s32[256,1]{0,1:T(1,128)S(1)} %compare_select_fusion) | copy-start | bytes 3076
  17.7 0.7 copy-start.4
  22.3 6.2 %copy-start.33 = (f32[1,128,2]{1,2,0:T(2,128)S(1)}, f32[1,128,2]{1,2,0:T(2,128)}, u32[]{:S(2)}) copy-start(f32[1,128,2]{1,2,0:T(2,128)} %param.10) | copy-start | bytes 3076
  22.3 6.5 %copy-start.3 = (bf16[1,128,1024]{2,1,0:T(8,128)(2,1)S(1)}, bf16[1,128,1024]{2,1,0:T(8,128)(2,1)}, u32[]{:S(2)}) copy-start(bf16[1,128,1024]{2,1,0:T(8,128)(2,1)} %param.13) | copy-start | bytes 786436
  22.3 55.7 %all-to-all-start = ((bf16[32,32,1024]{2,1,0:T(8,128)(2,1)}), bf16[32,32,1024]{2,1,0:T(8,128)(2,1)S(1)}, u32[]{:S(2)}, u32[]{:S(2)}) async-start(bf16[32,32,1024]{2,1,0:T(8,128)(2,1)} %bitcast.37), calls=%async_computation | async-start | bytes 4194304 | tf_op jit(solution)/shard_map/all_to_all | solution.py:83
  78.0 6.9 %copy-start.2 = (bf16[32,32,1024]{2,1,0:T(8,128)(2,1)}, bf16[32,32,1024]{2,1,0:T(8,128)(2,1)S(1)}, u32[]{:S(2)}) copy-start(bf16[32,32,1024]{2,1,0:T(8,128)(2,1)S(1)} %all-to-all-done) | copy-start | bytes 6291460
  80.9 53.5 %all-to-all-start.2 = ((bf16[32,32,1024]{2,1,0:T(8,128)(2,1)}), bf16[32,32,1024]{2,1,0:T(8,128)(2,1)}, u32[]{:S(2)}, u32[]{:S(2)}) async-start(bf16[32,32,1024]{2,1,0:T(8,128)(2,1)} %bitcast.51), calls=%async_computation.2 | async-start | bytes 4194304 | tf_op jit(solution)/shard_map/all_to_all | solution.py:84
  134.5 5.2 %copy-start = (bf16[4,1024,512]{2,1,0:T(8,128)(2,1)S(1)}, bf16[4,1024,512]{2,1,0:T(8,128)(2,1)}, u32[]{:S(2)}) copy-start(bf16[4,1024,512]{2,1,0:T(8,128)(2,1)} %param.11) | copy-start | bytes 12582916
  142.5 53.3 %all-to-all-start.3 = ((bf16[32,32,1024]{2,1,0:T(8,128)(2,1)}), bf16[32,32,1024]{2,1,0:T(8,128)(2,1)S(1)}, u32[]{:S(2)}, u32[]{:S(2)}) async-start(bf16[32,32,1024]{2,1,0:T(8,128)(2,1)} %bitcast.157), calls=%async_computation.3 | async-start | bytes 4194304 | tf_op jit(solution)/shard_map/all_to_all | solution.py:43
  195.8 1.4 copy-start.1
  197.2 53.3 %all-to-all-start.1 = ((bf16[32,32,1024]{2,1,0:T(8,128)(2,1)}), bf16[32,32,1024]{2,1,0:T(8,128)(2,1)S(1)}, u32[]{:S(2)}, u32[]{:S(2)}) async-start(bf16[32,32,1024]{2,1,0:T(8,128)(2,1)} %bitcast.150), calls=%async_computation.1 | async-start | bytes 4194304 | tf_op jit(solution)/shard_map/all_to_all | solution.py:43
  201.0 6.5 %copy-start.6 = (f32[4,32,8,512]{3,2,1,0:T(8,128)S(1)}, f32[4,32,8,512]{3,2,1,0:T(8,128)}, u32[]{:S(2)}) copy-start(f32[4,32,8,512]{3,2,1,0:T(8,128)} %fusion.2) | copy-start | bytes 6291460
  217.2 4.1 %copy-start.7 = (f32[1,128,1024]{2,1,0:T(8,128)S(1)}, f32[1,128,1024]{2,1,0:T(8,128)}, u32[]{:S(2)}) copy-start(f32[1,128,1024]{2,1,0:T(8,128)} %get-tuple-element.5) | copy-start | bytes 1572868
  221.6 4.2 %copy-start.8 = (bf16[1,128,1024]{2,1,0:T(8,128)(2,1)}, bf16[1,128,1024]{2,1,0:T(8,128)(2,1)S(1)}, u32[]{:S(2)}) copy-start(bf16[1,128,1024]{2,1,0:T(8,128)(2,1)S(1)} %multiply_convert_fusion.2) | copy-start | bytes 786436
  222.3 32.9 %collective-permute-start.2 = (bf16[1,15,1024]{2,1,0:T(8,128)(2,1)}, bf16[1,15,1024]{2,1,0:T(8,128)(2,1)}, u32[]{:S(2)}, u32[]{:S(2)}) collective-permute-start(bf16[1,15,1024]{2,1,0:T(8,128)(2,1)} %get-tuple-element.6), channel_id=1, source_target_pairs={{0,8},{8,16},{16,24},{1,9},{9,17},{17,25},{2,10},{10,18},{18,26},{... | collective-permute-start | bytes 92168 | tf_op jit(solution)/shard_map/ppermute | solution.py:15
  225.8 29.4 %collective-permute-start.3 = (bf16[1,15,1024]{2,1,0:T(8,128)(2,1)}, bf16[1,15,1024]{2,1,0:T(8,128)(2,1)}, u32[]{:S(2)}, u32[]{:S(2)}) collective-permute-start(bf16[1,15,1024]{2,1,0:T(8,128)(2,1)} %get-tuple-element.7), channel_id=1, source_target_pairs={{8,0},{16,8},{24,16},{9,1},{17,9},{25,17},{10,2},{18,10},{26,18},{... | collective-permute-start | bytes 92168 | tf_op jit(solution)/shard_map/ppermute | solution.py:18
  252.3 2.1 copy-start.5
  252.3 2.9 %copy-start.9 = (bf16[1,128,1024]{2,1,0:T(8,128)(2,1)S(1)}, bf16[1,128,1024]{2,1,0:T(8,128)(2,1)}, u32[]{:S(2)}) copy-start(bf16[1,128,1024]{2,1,0:T(8,128)(2,1)} %copy-done.8) | copy-start | bytes 786436
  253.0 3.1 %copy-start.12 = (f32[1,1024]{1,0:T(1,128)S(1)}, f32[1,1024]{1,0:T(1,128)}, u32[]{:S(2)}) copy-start(f32[1,1024]{1,0:T(1,128)} %copy-done.11) | copy-start | bytes 12292
  253.0 3.1 %copy-start.14 = (f32[1,1024]{1,0:T(1,128)S(1)}, f32[1,1024]{1,0:T(1,128)}, u32[]{:S(2)}) copy-start(f32[1,1024]{1,0:T(1,128)} %copy-done.13) | copy-start | bytes 12292
  253.0 3.1 %copy-start.16 = (f32[1,1024]{1,0:T(1,128)S(1)}, f32[1,1024]{1,0:T(1,128)}, u32[]{:S(2)}) copy-start(f32[1,1024]{1,0:T(1,128)} %copy-done.15) | copy-start | bytes 12292
  253.0 3.1 %copy-start.18 = (f32[1,1024]{1,0:T(1,128)S(1)}, f32[1,1024]{1,0:T(1,128)}, u32[]{:S(2)}) copy-start(f32[1,1024]{1,0:T(1,128)} %copy-done.17) | copy-start | bytes 12292
  253.0 3.1 %copy-start.20 = (f32[1,1024]{1,0:T(1,128)S(1)}, f32[1,1024]{1,0:T(1,128)}, u32[]{:S(2)}) copy-start(f32[1,1024]{1,0:T(1,128)} %copy-done.19) | copy-start | bytes 12292
  253.0 3.1 %copy-start.22 = (f32[1,1024]{1,0:T(1,128)S(1)}, f32[1,1024]{1,0:T(1,128)}, u32[]{:S(2)}) copy-start(f32[1,1024]{1,0:T(1,128)} %copy-done.21) | copy-start | bytes 12292
  253.0 3.1 %copy-start.24 = (f32[1,1024]{1,0:T(1,128)S(1)}, f32[1,1024]{1,0:T(1,128)}, u32[]{:S(2)}) copy-start(f32[1,1024]{1,0:T(1,128)} %copy-done.23) | copy-start | bytes 12292
  253.0 3.1 %copy-start.26 = (f32[1,1024]{1,0:T(1,128)S(1)}, f32[1,1024]{1,0:T(1,128)}, u32[]{:S(2)}) copy-start(f32[1,1024]{1,0:T(1,128)} %copy-done.25) | copy-start | bytes 12292
  253.0 3.1 %copy-start.28 = (f32[1,1024]{1,0:T(1,128)S(1)}, f32[1,1024]{1,0:T(1,128)}, u32[]{:S(2)}) copy-start(f32[1,1024]{1,0:T(1,128)} %copy-done.27) | copy-start | bytes 12292
  253.0 3.1 %copy-start.30 = (f32[1,1024]{1,0:T(1,128)S(1)}, f32[1,1024]{1,0:T(1,128)}, u32[]{:S(2)}) copy-start(f32[1,1024]{1,0:T(1,128)} %copy-done.29) | copy-start | bytes 12292
  253.1 3.1 %copy-start.32 = (f32[1,1024]{1,0:T(1,128)S(1)}, f32[1,1024]{1,0:T(1,128)}, u32[]{:S(2)}) copy-start(f32[1,1024]{1,0:T(1,128)} %copy-done.31) | copy-start | bytes 12292
where the time goes:
time: 261 us; the launch traced here: 259 us
  waiting for transfers between devices  153 us (59%)
  starting transfers between devices  29.9 us (11%)
  matrix products  28.2 us (11%)
  local copies, waits for them, and re-layouts  26.9 us (10%)
  other arithmetic  20.2 us (8%)
    all_to_all x2, waiting for transfers between devices, to_sources(): lax.all_to_all(whole_term, ('seq', 'exp'), split_axis=0, concat_axis=0, t...  64.3 us
    all_to_all x1, waiting for transfers between devices, per_device(): lax.all_to_all(wide_down, ('seq', 'exp'), split_axis=0, concat_axis=0, ti...  44.9 us
    all_to_all x1, waiting for transfers between devices, per_device(): lax.all_to_all(wide_up, ('seq', 'exp'), split_axis=0, concat_axis=0, tile...  43.3 us
    ppermute x2, starting transfers between devices, extended(): lax.ppermute(lax.slice_in_dim(block, block.shape[dim] - width, None, axis...  8.07 us
    all_to_all x2, starting transfers between devices, to_sources(): lax.all_to_all(whole_term, ('seq', 'exp'), split_axis=0, concat_axis=0, t...  7.66 us
    dot_general x1, matrix products, per_device(): jnp.einsum('gecd,gech->edh', routed_up, pre_grad, preferred_element_type=...  6.44 us
    dot_general x1, matrix products, per_device(): jnp.einsum('gech,gecd->ehd', activation, routed_down, preferred_element_t...  6.38 us
    all_to_all x1, starting transfers between devices, per_device(): lax.all_to_all(wide_up, ('seq', 'exp'), split_axis=0, concat_axis=0, tile...  6.2 us
  transfers between devices with their start and end apart: 8, of which 4 were waited for; matrix products, arithmetic and copies ran while one was open for 19% of the time, Pallas kernels for 0%

commit v1 on v0

v1 whole, which is shorter than its diff:
```python
import jax
import jax.numpy as jnp
from jax import lax
from jax.sharding import PartitionSpec as P

KERNEL = 31
CAP = 8
BF16 = jnp.bfloat16
F32 = jnp.float32


def silu_slope(values):
    logistic = jax.nn.sigmoid(values)
    return logistic * (1.0 + values * (1.0 - logistic))


def edge_rows(block):
    width = (KERNEL - 1) // 2
    count = lax.axis_size("seq")
    forward = [(i, i + 1) for i in range(count - 1)]
    backward = [(target, source) for source, target in forward]
    low = lax.ppermute(block[-width:], "seq", forward)
    high = lax.ppermute(block[:width], "seq", backward)
    return jnp.concatenate([low, block, high], axis=0)


def local_conv(padded, kernel, reverse, length):
    margin = (KERNEL - 1) // 2
    summed = jnp.zeros((length, padded.shape[1]), F32)
    for tap_index in range(KERNEL):
        offset = 2 * margin - tap_index if reverse else tap_index
        summed = summed + kernel[tap_index] * padded[offset : offset + length]
    return summed


def per_device(frames, conv_kernel, routes, gates, w_in, w_out, cotangent):
    n_seq = lax.axis_size("seq")
    n_exp = lax.axis_size("exp")
    experts = w_in.shape[0]
    length = frames.shape[1]
    width = frames.shape[2]
    slots = experts * n_exp * CAP
    per_dest = experts * CAP

    ids = routes[0].reshape(2 * length)
    order = jnp.arange(2 * length, dtype=jnp.int32)
    earlier = (ids[:, None] == ids[None, :]) & (order[None, :] < order[:, None])
    places = ids * CAP + jnp.sum(earlier.astype(jnp.int32), axis=1)
    places = places.reshape(length, 2)
    gate_pair = gates[0]
    slot_ids = jnp.arange(slots, dtype=jnp.int32)
    picks = [(places[:, k][:, None] == slot_ids[None, :]) for k in range(2)]
    either = (picks[0] | picks[1]).astype(BF16)
    slot_gate = sum(jnp.sum(jnp.where(picks[k], gate_pair[:, k][:, None], 0.0), axis=0) for k in range(2))

    mixing = local_conv(edge_rows(frames[0]).astype(F32), conv_kernel, False, length)
    hidden = (frames[0].astype(F32) + jax.nn.silu(mixing)).astype(BF16)

    def to_slots(rows):
        return jnp.einsum("ts,td->sd", either, rows, preferred_element_type=F32)

    up = to_slots(hidden).astype(BF16)
    down = (slot_gate[:, None] * to_slots(cotangent[0])).astype(BF16)
    both = jnp.concatenate([up, down], axis=1).reshape(n_exp, per_dest, 2 * width)
    got = lax.all_to_all(both, "exp", split_axis=0, concat_axis=0, tiled=True)
    got = lax.all_gather(got, "seq", axis=0, tiled=False)
    got = got.reshape(n_seq * n_exp, experts, CAP, 2 * width).transpose(1, 0, 2, 3)
    got = got.reshape(experts, n_seq * n_exp * CAP, 2 * width)
    routed_up, routed_down = got[:, :, :width], got[:, :, width:]

    pre_act = jnp.einsum("erd,edh->erh", routed_up, w_in, preferred_element_type=F32)
    activation = jax.nn.silu(pre_act).astype(BF16)
    expert_out = jnp.einsum("erh,ehd->erd", activation, w_out, preferred_element_type=F32).astype(BF16)
    act_grad = jnp.einsum("erd,ehd->erh", routed_down, w_out, preferred_element_type=F32)
    pre_grad = (act_grad * silu_slope(pre_act)).astype(BF16)
    input_grad = jnp.einsum("erh,edh->erd", pre_grad, w_in, preferred_element_type=F32).astype(BF16)
    back = jnp.concatenate([expert_out, input_grad], axis=2)
    back = back.reshape(experts, n_seq, n_exp, CAP, 2 * width).transpose(1, 2, 0, 3, 4)
    back = back.reshape(n_seq, n_exp * per_dest, 2 * width)
    back = lax.psum_scatter(back, "seq", scatter_dimension=0, tiled=False)
    back = back.reshape(n_exp, per_dest, 2 * width)
    back = lax.all_to_all(back, "exp", split_axis=0, concat_axis=0, tiled=True)
    back = back.reshape(slots, 2 * width)

    w_out_grad = jnp.einsum("erh,erd->ehd", activation, routed_down, preferred_element_type=F32)
    w_in_grad = jnp.einsum("erd,erh->edh", routed_up, pre_grad, preferred_element_type=F32)

    mixed = hidden.astype(F32)
    for k in range(2):
        picked = jnp.dot(picks[k].astype(BF16), back[:, :width], preferred_element_type=F32)
        mixed = mixed + gate_pair[:, k][:, None] * picked
    hidden_grad = cotangent[0].astype(F32) + jnp.dot(either, back[:, width:], preferred_element_type=F32)
    conv_back = (hidden_grad * silu_slope(mixing)).astype(BF16)
    spread = local_conv(edge_rows(conv_back).astype(F32), conv_kernel, True, length)
    frames_grad = (hidden_grad + spread).astype(BF16)
    return (mixed.astype(BF16)[None], frames_grad[None], w_in_grad, w_out_grad)


def solution(mesh):
    rows = P("exp", "seq", None)
    in_specs = (rows, P(), rows, rows, P("exp", None, "seq"), rows, rows)
    out_specs = (rows, rows, P("exp", None, "seq"), rows)
    return jax.shard_map(
        per_device, mesh=mesh, in_specs=in_specs, out_specs=out_specs, check_vma=False
    )
```

time: 261 us -> 198 us (0.76)
  waiting for transfers between devices: 153 us -> 94.2 us
  blocking collectives: 0 us -> 30.2 us
  other arithmetic: 20.2 us -> 7.18 us
  local copies, waits for them, and re-layouts: 26.9 us -> 13.9 us
  between operations: 1.35 us -> 14.3 us
  starting transfers between devices: 29.9 us -> 17.9 us
  matrix products: 28.2 us -> 20 us
    all_to_all x4 -> x1, waiting for transfers between devices: 152 us -> 13.4 us  [per_device(): back = lax.all_to_all(back, 'exp', split_axis=0, concat_axis=0, tiled=True)]
    reduce_scatter x0 -> x1, waiting for transfers between devices: none -> 44.3 us  [per_device(): back = lax.psum_scatter(back, 'seq', scatter_dimension=0, tiled=False)]
    all_gather x0 -> x1, waiting for transfers between devices: none -> 34.2 us  [per_device(): got = lax.all_gather(got, 'seq', axis=0, tiled=False)]
    all_to_all x0 -> x1, blocking collectives: none -> 30.2 us  [per_device(): got = lax.all_to_all(both, 'exp', split_axis=0, concat_axis=0, tiled=True)]
    all_to_all x4 -> x1, starting transfers between devices: 17.7 us -> 5.23 us  [per_device(): back = lax.all_to_all(back, 'exp', split_axis=0, concat_axis=0, tiled=True)]
    dot_general x6 -> x11, matrix products: 28.2 us -> 20 us  [the longest x1 6.44 us: per_device(): jnp.einsum('erd,erh->edh', routed_up, pre_grad, preferred_element_type=F32)]
    reduce_sum x5 -> x2, other arithmetic: 6.37 us -> 0.33 us  [the longest x1 0.18 us: per_device(): places = ids * CAP + jnp.sum(earlier.astype(jnp.int32), axis=1)]
    broadcast_in_dim x4 -> x1, local copies, waits for them, and re-layouts: 6.17 us -> 0.76 us  [per_device(): jnp.where(picks[k], gate_pair[:, k][:, None], 0.0)]
  transfers between devices with their start and end apart: 8 -> 7, of which waited for: 4 -> 4; matrix products, arithmetic and copies ran while one was open for 19% -> 9% of each run, Pallas kernels for 0% -> 0%
where the time goes in v1:
time: 198 us
  waiting for transfers between devices  94.2 us (48%)
  blocking collectives  30.2 us (15%)
  matrix products  20 us (10%)
  starting transfers between devices  17.9 us (9%)
  between operations  14.3 us (7%)
  local copies, waits for them, and re-layouts  13.9 us (7%)
  other arithmetic  7.18 us (4%)
    reduce_scatter x1, waiting for transfers between devices, per_device(): back = lax.psum_scatter(back, 'seq', scatter_dimension=0, tiled=False)  44.3 us
    all_gather x1, waiting for transfers between devices, per_device(): got = lax.all_gather(got, 'seq', axis=0, tiled=False)  34.2 us
    all_to_all x1, blocking collectives, per_device(): got = lax.all_to_all(both, 'exp', split_axis=0, concat_axis=0, tiled=True)  30.2 us
    all_to_all x1, waiting for transfers between devices, per_device(): back = lax.all_to_all(back, 'exp', split_axis=0, concat_axis=0, tiled=True)  13.4 us
    ppermute x2, starting transfers between devices, edge_rows(): low = lax.ppermute(block[-width:], 'seq', forward)  8.72 us
    dot_general x1, matrix products, per_device(): jnp.einsum('erd,erh->edh', routed_up, pre_grad, preferred_element_type=F32)  6.44 us
    all_to_all x1, starting transfers between devices, per_device(): back = lax.all_to_all(back, 'exp', split_axis=0, concat_axis=0, tiled=True)  5.23 us
    dot_general x1, matrix products, per_device(): jnp.einsum('erh,erd->ehd', activation, routed_down, preferred_element_typ...  4.74 us
  transfers between devices with their start and end apart: 7, of which 4 were waited for; matrix products, arithmetic and copies ran while one was open for 9% of the time, Pallas kernels for 0%

profile of v1, /device:TPU:1, one launch (start us, length us, event | category | flops | bytes accessed | tf_op | source)
XLA Modules:
  0.0 197.6 jit_solution(5247712387468983119)
XLA Ops:
  7.2 0.0 copy-start.3
  7.2 0.0 all-gather.3.cloned.1.call-start
  7.2 0.8 slice_bitcast_fusion.1
  8.0 4.5 %collective-permute-start = (bf16[15,1024]{1,0:T(8,128)(2,1)S(1)}, bf16[15,1024]{1,0:T(8,128)(2,1)S(1)}, u32[]{:S(2)}, u32[]{:S(2)}) collective-permute-start(bf16[15,1024]{1,0:T(8,128)(2,1)S(1)} %get-tuple-element.10), channel_id=1, source_target_pairs={{0,8},{8,16},{16,24},{1,9},{9,17},{17,25},{2,10},{10,18},{18,26},{... | collective-permute-start | bytes 92168 | tf_op jit(solution)/shard_map/ppermute | solution.py:22
  12.6 1.9 collective-permute-start.1
  14.5 0.8 slice_bitcast_fusion.2
  15.3 0.8 copy.32
  16.1 0.1 eq.45
  16.2 0.2 convert_reduce_fusion
  16.4 0.1 reduce_sum.30
  16.6 0.2 slice_reduce_fusion
  16.7 1.4 fusion.97
  18.2 0.1 select_reduce_fusion
  18.3 1.4 fusion.8
  19.7 1.1 fusion.98
  20.9 1.0 maximum_convert_fusion
  21.9 2.2 %add_convert_fusion = (bf16[128,1024]{1,0:T(8,128)(2,1)S(1)}, f32[128,1024]{1,0:T(8,128)S(1)}) fusion(bf16[1,128,1024]{2,1,0:T(8,128)(2,1)S(1)} %copy-done.3, f32[158,1024]{1,0:T(8,128)S(1)} %maximum_convert_fusion, f32[1024]{0:T(1024)S(1)} %bitcast.139, f32[1024]{0:T(1024)S(1)} %bitcast.141, f32[1024]{0:T(1024)S(1)} %bitcast.83, f32[1024]{0:T(1024)S(1)} %bitcast.85, ...), kind=kLoop, calls=%fused_computation.152 | loop fusion | flops 8912896 | bytes 17428480 | tf_op jit(solution)/shard_map/convert_element_type | solution.py:57
  24.2 0.4 convolution_convert_fusion.2
  24.6 0.1 pad_maximum_fusion.1
  24.6 30.2 %all_to_all.10 = bf16[8,32,2048]{2,1,0:T(8,128)(2,1)} all-to-all(bf16[8,32,2048]{2,1,0:T(8,128)(2,1)S(1)} %bitcast.78), channel_id=1, replica_groups=mesh['seq'=4,'exp'=8] {'exp'}, dimensions={0} | all-to-all | bytes 2097152 | tf_op jit(solution)/shard_map/all_to_all | solution.py:65
  54.9 0.0 all-gather.3.cloned.1.call-update
  54.9 0.0 reduce-scatter.2.cloned.1.call-start
  55.0 34.2 %all-gather.3.cloned.1.call-done = bf16[32,32,2048]{2,1,0:T(8,128)(2,1)} async-done(((bf16[8,32,2048]{2,1,0:T(8,128)(2,1)}), bf16[32,32,2048]{2,1,0:T(8,128)(2,1)}) %all-gather.3.cloned.1.call-update) | async-done | bytes 4194320 | tf_op jit(solution)/shard_map/all_gather | solution.py:66
  89.1 2.7 %copy_bitcast_fusion = bf16[4,256,2048]{2,1,0:T(8,128)(2,1)S(1)} fusion(bf16[32,32,2048]{2,1,0:T(8,128)(2,1)} %all-gather.3.cloned.1.call-done), kind=kLoop, calls=%fused_computation.1 | loop fusion | bytes 8388608 | tf_op jit(solution)/shard_map/reshape | solution.py:68
  91.8 0.8 copy-done.2
  92.6 1.2 fusion.6
  93.8 0.9 copy-done
  94.7 1.6 copy-done.5
  96.3 1.7 multiply_convert_fusion
  98.0 1.3 convolution_convert_fusion.1
  99.3 1.3 convolution_convert_fusion
  100.6 0.4 pad_maximum_fusion
  101.0 2.6 %copy.35 = bf16[4,4,8,8,2048]{4,3,0,2,1:T(8,128)(2,1)} copy(bf16[4,4,8,8,2048]{4,3,2,1,0:T(8,128)(2,1)S(1)} %bitcast.74) | data formatting | bytes 8388608 | tf_op jit(solution)/shard_map/reshape | solution.py:78
  103.6 0.0 reduce-scatter.2.cloned.1.call-update
  103.6 44.3 %reduce-scatter.2.cloned.1.call-done = bf16[1,256,2048]{2,1,0:T(8,128)(2,1)} async-done(((bf16[4,256,2048]{2,1,0:T(8,128)(2,1)}), bf16[1,256,2048]{2,1,0:T(8,128)(2,1)}) %reduce-scatter.2.cloned.1.call-update) | async-done | bytes 1048592 | tf_op jit(solution)/shard_map/reduce_scatter | solution.py:80
  147.9 5.2 %all-to-all-start.1 = ((bf16[8,32,2048]{2,1,0:T(8,128)(2,1)}), bf16[8,32,2048]{2,1,0:T(8,128)(2,1)S(1)}, u32[]{:S(2)}, u32[]{:S(2)}) async-start(bf16[8,32,2048]{2,1,0:T(8,128)(2,1)} %bitcast.80), calls=%async_computation.2 | async-start | bytes 2097152 | tf_op jit(solution)/shard_map/all_to_all | solution.py:82
  153.1 6.4 %fusion.4 = f32[4,1024,512]{2,1,0:T(8,128)} fusion(bf16[4,256,512]{2,1,0:T(8,128)(2,1)S(1)} %multiply_convert_fusion, bf16[4,256,2048]{2,1,0:T(8,128)(2,1)} %copy-done), kind=kOutput, calls=%fused_computation.11 | convolution fusion | flops 1073741824 | bytes 11534336 | tf_op jit(solution)/shard_map/erd,erh->edh/dot_general | solution.py:86
  159.6 4.7 %fusion = f32[4,512,1024]{2,1,0:T(8,128)} fusion(bf16[4,256,2048]{2,1,0:T(8,128)(2,1)S(1)} %copy-done.1, f32[4,256,512]{2,1,0:T(8,128)S(1)} %copy-done.7), kind=kOutput, calls=%fused_computation.7 | convolution fusion | flops 1076363264 | bytes 12582912 | tf_op jit(solution)/shard_map/erh,erd->ehd/dot_general | solution.py:85
  164.3 13.4 %all-to-all-done.1 = bf16[8,32,2048]{2,1,0:T(8,128)(2,1)S(1)} async-done(((bf16[8,32,2048]{2,1,0:T(8,128)(2,1)}), bf16[8,32,2048]{2,1,0:T(8,128)(2,1)S(1)}, u32[]{:S(2)}, u32[]{:S(2)}) %all-to-all-start.1) | async-done | bytes 1048608 | tf_op jit(solution)/shard_map/all_to_all | solution.py:82
  177.7 0.3 fusion.10
  178.0 0.3 convolution_add_fusion
  178.3 0.2 multiply_convert_fusion.2
  178.5 4.2 %collective-permute-start.2 = (bf16[15,1024]{1,0:T(8,128)(2,1)S(1)}, bf16[15,1024]{1,0:T(8,128)(2,1)S(1)}, u32[]{:S(2)}, u32[]{:S(2)}) collective-permute-start(bf16[15,1024]{1,0:T(8,128)(2,1)S(1)} %get-tuple-element.8), channel_id=1, source_target_pairs={{0,8},{8,16},{16,24},{1,9},{9,17},{17,25},{2,10},{10,18},{18,26},{... | collective-permute-start | bytes 92168 | tf_op jit(solution)/shard_map/ppermute | solution.py:22
  182.7 1.9 collective-permute-start.3
  184.7 1.0 fusion.12
  185.6 2.3 %collective-permute-done.3 = bf16[15,1024]{1,0:T(8,128)(2,1)S(1)} collective-permute-done((bf16[15,1024]{1,0:T(8,128)(2,1)S(1)}, bf16[15,1024]{1,0:T(8,128)(2,1)S(1)}, u32[]{:S(2)}, u32[]{:S(2)}) %collective-permute-start.3) | collective-permute-done | bytes 30752 | tf_op jit(solution)/shard_map/ppermute | solution.py:23
  188.0 0.1 maximum_convert_fusion.1
  188.0 2.8 %fusion.82 = bf16[1,128,1024]{2,1,0:T(8,128)(2,1)} fusion(f32[128,1024]{1,0:T(8,128)S(1)} %convolution_add_fusion, f32[158,1024]{1,0:T(8,128)S(1)} %maximum_convert_fusion.1, f32[1024]{0:T(1024)S(1)} %bitcast.140, f32[1024]{0:T(1024)S(1)} %bitcast.142, f32[1024]{0:T(1024)S(1)} %bitcast.84, f32[1024]{0:T(1024)S(1)} %bitcast.86, f32[1024]{0:T(1024)S(1)} %bitcast.88, ...), kind=kLoop, calls=%fused_computation.162 | loop fusion | flops 8257536 | bytes 17166336 | tf_op jit(solution)/shard_map/broadcast_in_dim | solution.py:96
  (18 shorter events, 0.1 us)
Async XLA Ops:
  7.2 14.7 %copy-start.3 = (bf16[1,128,1024]{2,1,0:T(8,128)(2,1)S(1)}, bf16[1,128,1024]{2,1,0:T(8,128)(2,1)}, u32[]{:S(2)}) copy-start(bf16[1,128,1024]{2,1,0:T(8,128)(2,1)} %param.7) | copy-start | bytes 786436
  7.2 81.9 %all-gather.3.cloned.1.call-start = ((), (), s32[]{:S(2)}) async-start(), calls=%async_computation.4 | async-start | bytes 5242880 | tf_op jit(solution)/shard_map/all_gather | solution.py:66
  8.0 12.8 %collective-permute-start = (bf16[15,1024]{1,0:T(8,128)(2,1)S(1)}, bf16[15,1024]{1,0:T(8,128)(2,1)S(1)}, u32[]{:S(2)}, u32[]{:S(2)}) collective-permute-start(bf16[15,1024]{1,0:T(8,128)(2,1)S(1)} %get-tuple-element.10), channel_id=1, source_target_pairs={{0,8},{8,16},{16,24},{1,9},{9,17},{17,25},{2,10},{10,18},{18,26},{... | collective-permute-start | bytes 92168 | tf_op jit(solution)/shard_map/ppermute | solution.py:22
  12.6 8.3 %collective-permute-start.1 = (bf16[15,1024]{1,0:T(8,128)(2,1)S(1)}, bf16[15,1024]{1,0:T(8,128)(2,1)S(1)}, u32[]{:S(2)}, u32[]{:S(2)}) collective-permute-start(bf16[15,1024]{1,0:T(8,128)(2,1)S(1)} %get-tuple-element.11), channel_id=1, source_target_pairs={{8,0},{16,8},{24,16},{9,1},{17,9},{25,17},{10,2},{18,10},{26,18},{... | collective-permute-start | bytes 92168 | tf_op jit(solution)/shard_map/ppermute | solution.py:23
  54.9 93.0 %reduce-scatter.2.cloned.1.call-start = ((), (), s32[]{:S(2)}) async-start(), calls=%async_computation.3 | async-start | bytes 5242880 | tf_op jit(solution)/shard_map/reduce_scatter | solution.py:80
  89.1 3.4 %copy-start.2 = (bf16[4,1024,512]{2,1,0:T(8,128)(2,1)S(1)}, bf16[4,1024,512]{2,1,0:T(8,128)(2,1)}, u32[]{:S(2)}) copy-start(bf16[4,1024,512]{2,1,0:T(8,128)(2,1)} %param.11) | copy-start | bytes 12582916
  92.6 2.1 %copy-start = (bf16[4,256,2048]{2,1,0:T(8,128)(2,1)}, bf16[4,256,2048]{2,1,0:T(8,128)(2,1)S(1)}, u32[]{:S(2)}) copy-start(bf16[4,256,2048]{2,1,0:T(8,128)(2,1)S(1)} %copy_bitcast_fusion) | copy-start | bytes 12582916
  92.6 3.7 %copy-start.5 = (bf16[4,512,1024]{2,1,0:T(8,128)(2,1)S(1)}, bf16[4,512,1024]{2,1,0:T(8,128)(2,1)}, u32[]{:S(2)}) copy-start(bf16[4,512,1024]{2,1,0:T(8,128)(2,1)} %param.12) | copy-start | bytes 12582916
  96.3 1.7 copy-start.6
  147.9 29.8 %all-to-all-start.1 = ((bf16[8,32,2048]{2,1,0:T(8,128)(2,1)}), bf16[8,32,2048]{2,1,0:T(8,128)(2,1)S(1)}, u32[]{:S(2)}, u32[]{:S(2)}) async-start(bf16[8,32,2048]{2,1,0:T(8,128)(2,1)} %bitcast.80), calls=%async_computation.2 | async-start | bytes 2097152 | tf_op jit(solution)/shard_map/all_to_all | solution.py:82
  153.1 6.5 %copy-start.1 = (bf16[4,256,2048]{2,1,0:T(8,128)(2,1)S(1)}, bf16[4,256,2048]{2,1,0:T(8,128)(2,1)}, u32[]{:S(2)}) copy-start(bf16[4,256,2048]{2,1,0:T(8,128)(2,1)} %copy-done) | copy-start | bytes 12582916
  153.1 6.5 %copy-start.7 = (f32[4,256,512]{2,1,0:T(8,128)S(1)}, f32[4,256,512]{2,1,0:T(8,128)}, u32[]{:S(2)}) copy-start(f32[4,256,512]{2,1,0:T(8,128)} %copy-done.6) | copy-start | bytes 6291460
  159.6 18.4 %copy-start.4 = (bf16[1,128,1024]{2,1,0:T(8,128)(2,1)S(1)}, bf16[1,128,1024]{2,1,0:T(8,128)(2,1)}, u32[]{:S(2)}) copy-start(bf16[1,128,1024]{2,1,0:T(8,128)(2,1)} %param.13) | copy-start | bytes 786436
  178.5 7.1 %collective-permute-start.2 = (bf16[15,1024]{1,0:T(8,128)(2,1)S(1)}, bf16[15,1024]{1,0:T(8,128)(2,1)S(1)}, u32[]{:S(2)}, u32[]{:S(2)}) collective-permute-start(bf16[15,1024]{1,0:T(8,128)(2,1)S(1)} %get-tuple-element.8), channel_id=1, source_target_pairs={{0,8},{8,16},{16,24},{1,9},{9,17},{17,25},{2,10},{10,18},{18,26},{... | collective-permute-start | bytes 92168 | tf_op jit(solution)/shard_map/ppermute | solution.py:22
  182.7 5.2 %collective-permute-start.3 = (bf16[15,1024]{1,0:T(8,128)(2,1)S(1)}, bf16[15,1024]{1,0:T(8,128)(2,1)S(1)}, u32[]{:S(2)}, u32[]{:S(2)}) collective-permute-start(bf16[15,1024]{1,0:T(8,128)(2,1)S(1)} %get-tuple-element.9), channel_id=1, source_target_pairs={{8,0},{16,8},{24,16},{9,1},{17,9},{25,17},{10,2},{18,10},{26,18},{... | collective-permute-start | bytes 92168 | tf_op jit(solution)/shard_map/ppermute | solution.py:23
Sparse Core Ops, SparseCore 0:
  55.0 34.0 all-gather.2
  103.8 44.1 reduce-scatter.1

commit v2 on v1

--- a/solution.py
+++ b/solution.py
@@ -1,6 +1,10 @@
+import functools
+
 import jax
 import jax.numpy as jnp
 from jax import lax
+from jax.experimental import pallas as pl
+from jax.experimental.pallas import tpu as pltpu
 from jax.sharding import PartitionSpec as P
 
 KERNEL = 31
@@ -31,6 +35,301 @@
         offset = 2 * margin - tap_index if reverse else tap_index
         summed = summed + kernel[tap_index] * padded[offset : offset + length]
     return summed
+
+
+GROUP = 8
+MESH = pl.DeviceIdType.MESH
+LAST = (((1,), (1,)), ((), ()))
+
+
+def expert_kernel(
+    n_seq, n_exp, send_ref, sort_ref, unsort_ref, w_in_hbm, w_out_hbm,
+    back_ref, rows_hbm, act_hbm, pre_hbm,
+    held, rows, acts, pres, mate_got, y_got, w_in_ref, w_out_ref,
+    exp_send, exp_recv, y_send, y_recv, mate_send, mate_recv,
+    back_send, back_recv, y_sum_send, y_sum_recv, pair_send, pair_recv, local_sem,
+):
+    n_y = n_seq // 2
+    experts, row_count, double = rows.shape
+    width = double // 2
+    block = experts * CAP
+    group_rows = GROUP * block
+    me_s, me_e = lax.axis_index("seq"), lax.axis_index("exp")
+    me_y, me_c = me_s // 2, me_s % 2
+    mate = me_y * 2 + 1 - me_c
+
+    def part(s, k):
+        return held.at[pl.ds(pl.multiple_of((s * n_exp + k) * block, block), block)]
+
+    def remote(src, dst, send, recv, s, e):
+        return pltpu.make_async_remote_copy(
+            src_ref=src, dst_ref=dst, send_sem=send, recv_sem=recv,
+            device_id=(s, e), device_id_type=MESH,
+        )
+
+    def same_core(y):
+        return lax.rem(y, n_y) * 2 + me_c
+
+    weights = [
+        pltpu.make_async_copy(w_in_hbm, w_in_ref, local_sem.at[0]),
+        pltpu.make_async_copy(w_out_hbm, w_out_ref, local_sem.at[1]),
+    ]
+
+    barrier = pltpu.get_barrier_semaphore()
+
+    def greet(s, e):
+        pl.semaphore_signal(barrier, inc=1, device_id=(s, e), device_id_type=MESH)
+
+    greet(mate, me_e)
+    for j in range(1, n_y):
+        greet(same_core(me_y + j), me_e)
+    for k in range(1, n_exp):
+        greet(me_s, lax.rem(me_e + k, n_exp))
+    pl.semaphore_wait(barrier, 1 + n_y - 1 + n_exp - 1)
+
+    def exp_copy(k):
+        target = lax.rem(me_e + k, n_exp)
+        return remote(
+            send_ref.at[target], part(me_s, k), exp_send.at[k], exp_recv.at[k], me_s, target
+        )
+
+    def y_copy(j, k):
+        spot = part(me_s, k)
+        return remote(
+            spot, spot, y_send.at[j, k], y_recv.at[j, k], same_core(me_y + j), me_e
+        )
+
+    def mate_copy(j, k):
+        spot = part(same_core(me_y + n_y - j), k)
+        return remote(spot, spot, mate_send.at[j, k], mate_recv.at[j, k], mate, me_e)
+
+    def loop(low, high, body):
+        def step(k, carry):
+            body(k)
+            return carry
+
+        lax.fori_loop(low, high, step, 0)
+
+    loop(1, n_exp, lambda k: exp_copy(k).start())
+    part(me_s, 0)[...] = send_ref[me_e]
+
+    def pass_on(k):
+        for j in range(1, n_y):
+            y_copy(j, k).start()
+        mate_copy(0, k).start()
+
+    def pass_far(k):
+        for j in range(1, n_y):
+            y_copy(j, k).wait_recv()
+            mate_copy(j, k).start()
+
+    pass_on(0)
+    for copy in weights:
+        copy.start()
+
+    def arrive(k):
+        exp_copy(k).wait_recv()
+        pass_on(k)
+
+        @pl.when(k >= 2)
+        def _():
+            pass_far(k - 2)
+
+    loop(1, n_exp, arrive)
+    pass_far(n_exp - 2)
+    pass_far(n_exp - 1)
+
+    def settle(k):
+        for j in range(n_y):
+            mate_copy(j, k).wait()
+        for j in range(1, n_y):
+            y_copy(j, k).wait_send()
+
+    loop(0, n_exp, settle)
+    loop(1, n_exp, lambda k: exp_copy(k).wait_send())
+
+    small = group_rows // experts
+    columns = 512
+
+    def sort(g):
+        span = pl.ds(pl.multiple_of(g * group_rows, group_rows), group_rows)
+        out_span = pl.ds(pl.multiple_of(g * small, small), small)
+        for col in range(0, double, columns):
+            cols = slice(col, col + columns)
+            placed = jnp.dot(
+                sort_ref[...], held[span, cols], preferred_element_type=F32
+            ).astype(BF16)
+            for n in range(experts):
+                rows[n, out_span, cols] = placed[n * small : (n + 1) * small]
+
+    groups = n_seq * n_exp // GROUP
+    loop(0, groups, sort)
+    rows_copy = pltpu.make_async_copy(rows, rows_hbm, local_sem.at[2])
+    rows_copy.start()
+    for copy in weights:
+        copy.wait()
+
+    tile = 256
+    tiles = row_count // tile
+
+    def hidden_units(i):
+        n, span = i // tiles, pl.ds(pl.multiple_of((i % tiles) * tile, tile), tile)
+        pre_act = jnp.dot(rows[n, span, :width], w_in_ref[n], preferred_element_type=F32)
+        act_grad = lax.dot_general(
+            rows[n, span, width:], w_out_ref[n], LAST, preferred_element_type=F32
+        )
+        logistic = jax.nn.sigmoid(pre_act)
+        acts[n, span, :] = (pre_act * logistic).astype(BF16)
+        pres[n, span, :] = (
+            act_grad * (logistic * (1.0 + pre_act * (1.0 - logistic)))
+        ).astype(BF16)
+
+    loop(0, experts * tiles, hidden_units)
+    act_copy = pltpu.make_async_copy(acts, act_hbm, local_sem.at[3])
+    pre_copy = pltpu.make_async_copy(pres, pre_hbm, local_sem.at[4])
+    act_copy.start()
+    pre_copy.start()
+    rows_copy.wait()
+
+    def partials(i):
+        n, span = i // tiles, pl.ds(pl.multiple_of((i % tiles) * tile, tile), tile)
+        rows[n, span, :width] = jnp.dot(
+            acts[n, span, :], w_out_ref[n], preferred_element_type=F32
+        ).astype(BF16)
+        rows[n, span, width:] = lax.dot_general(
+            pres[n, span, :], w_in_ref[n], LAST, preferred_element_type=F32
+        ).astype(BF16)
+
+    loop(0, experts * tiles, partials)
+
+    def unsort(g):
+        span = pl.ds(pl.multiple_of(g * group_rows, group_rows), group_rows)
+        in_span = pl.ds(pl.multiple_of(g * small, small), small)
+        for col in range(0, double, columns):
+            cols = slice(col, col + columns)
+            stacked = jnp.concatenate([rows[n, in_span, cols] for n in range(experts)], axis=0)
+            held[span, cols] = jnp.dot(
+                unsort_ref[...], stacked, preferred_element_type=F32
+            ).astype(BF16)
+
+    loop(0, groups, unsort)
+
+    def pair_copy(j, k):
+        y = lax.rem(me_y + j, n_y)
+        return remote(
+            part(y * 2 + 1 - me_c, k), mate_got.at[y, k],
+            pair_send.at[j, k], pair_recv.at[j, k], mate, me_e,
+        )
+
+    def y_sum_copy(j, k):
+        target = same_core(me_y + j)
+        return remote(
+            part(target, k), y_got.at[j - 1, k],
+            y_sum_send.at[j, k], y_sum_recv.at[j, k], target, me_e,
+        )
+
+    def home_copy(k):
+        return remote(
+            part(me_s, k), back_ref.at[me_e], back_send.at[k], back_recv.at[k],
+            me_s, lax.rem(me_e + n_exp - k, n_exp),
+        )
+
+    def order(i):
+        return lax.rem(i + 1, n_exp)
+
+    def pair_start(i):
+        for j in [*range(1, n_y), 0]:
+            pair_copy(j, order(i)).start()
+
+    def y_stage(i):
+        k = order(i)
+        for j in range(1, n_y):
+            pair_copy(j, k).wait_recv()
+            y = lax.rem(me_y + j, n_y)
+            spot = part(y * 2 + me_c, k)
+            spot[...] = (spot[...].astype(F32) + mate_got[y, k].astype(F32)).astype(BF16)
+            y_sum_copy(j, k).start()
+
+    def total(k):
+        pair_copy(0, k).wait_recv()
+        summed = part(me_s, k)[...].astype(F32) + mate_got[me_y, k].astype(F32)
+        for j in range(1, n_y):
+            y_sum_copy(j, k).wait_recv()
+            summed = summed + y_got[j - 1, k].astype(F32)
+        return summed.astype(BF16)
+
+    loop(0, n_exp, pair_start)
+    loop(0, n_exp, y_stage)
+
+    def home_stage(k):
+        part(me_s, k)[...] = total(k)
+        home_copy(k).start()
+
+    loop(1, n_exp, home_stage)
+    back_ref[me_e] = total(0)
+
+    def finish(k):
+        for j in range(n_y):
+            pair_copy(j, k).wait_send()
+        for j in range(1, n_y):
+            y_sum_copy(j, k).wait_send()
+
+    loop(0, n_exp, finish)
+
+    def come_home(k):
+        home_copy(k).wait_send()
+        pltpu.make_async_remote_copy(
+            src_ref=part(me_s, k), dst_ref=back_ref.at[lax.rem(me_e + k, n_exp)],
+            send_sem=back_send.at[k], recv_sem=back_recv.at[k],
+            device_id=(me_s, lax.rem(me_e + n_exp - k, n_exp)), device_id_type=MESH,
+        ).wait_recv()
+
+    loop(1, n_exp, come_home)
+    act_copy.wait()
+    pre_copy.wait()
+
+
+def run_experts(both, w_in, w_out):
+    n_seq, n_exp = lax.axis_size("seq"), lax.axis_size("exp")
+    experts, width, units = w_in.shape
+    block = experts * CAP
+    row_count = n_seq * n_exp * CAP
+    span = GROUP * block
+    spot = jnp.arange(span, dtype=jnp.int32)
+    expert, rest = spot // (GROUP * CAP), spot % (GROUP * CAP)
+    source = (rest // CAP) * block + expert * CAP + rest % CAP
+    sort = (source[:, None] == spot[None, :]).astype(BF16)
+    n_y = n_seq // 2
+    vmem, hbm = pl.BlockSpec(memory_space=pltpu.VMEM), pl.BlockSpec(memory_space=pl.ANY)
+    flat, pairs = pltpu.SemaphoreType.DMA((n_exp,)), pltpu.SemaphoreType.DMA((n_y, n_exp))
+    return pl.pallas_call(
+        functools.partial(expert_kernel, n_seq, n_exp),
+        out_shape=(
+            jax.ShapeDtypeStruct((n_exp, block, 2 * width), BF16),
+            jax.ShapeDtypeStruct((experts, row_count, 2 * width), BF16),
+            jax.ShapeDtypeStruct((experts, row_count, units), BF16),
+            jax.ShapeDtypeStruct((experts, row_count, units), BF16),
+        ),
+        in_specs=[vmem, vmem, vmem, hbm, hbm],
+        out_specs=(vmem, hbm, hbm, hbm),
+        scratch_shapes=[
+            pltpu.VMEM((n_seq * n_exp * block, 2 * width), BF16),
+            pltpu.VMEM((experts, row_count, 2 * width), BF16),
+            pltpu.VMEM((experts, row_count, units), BF16),
+            pltpu.VMEM((experts, row_count, units), BF16),
+            pltpu.VMEM((n_y, n_exp, block, 2 * width), BF16),
+            pltpu.VMEM((n_y - 1, n_exp, block, 2 * width), BF16),
+            pltpu.VMEM(w_in.shape, BF16),
+            pltpu.VMEM(w_out.shape, BF16),
+            flat, flat, pairs, pairs, pairs, pairs,
+            flat, flat, pairs, pairs, pairs, pairs,
+            pltpu.SemaphoreType.DMA((5,)),
+        ],
+        compiler_params=pltpu.CompilerParams(
+            collective_id=0, has_side_effects=True, vmem_limit_bytes=63 * 1024 * 1024
+        ),
+        name="expert_exchange",
+    )(both, sort, sort.T, w_in, w_out)
 
 
 def per_device(frames, conv_kernel, routes, gates, w_in, w_out, cotangent):
@@ -62,24 +361,8 @@
     up = to_slots(hidden).astype(BF16)
     down = (slot_gate[:, None] * to_slots(cotangent[0])).astype(BF16)
     both = jnp.concatenate([up, down], axis=1).reshape(n_exp, per_dest, 2 * width)
-    got = lax.all_to_all(both, "exp", split_axis=0, concat_axis=0, tiled=True)
-    got = lax.all_gather(got, "seq", axis=0, tiled=False)
-    got = got.reshape(n_seq * n_exp, experts, CAP, 2 * width).transpose(1, 0, 2, 3)
-    got = got.reshape(experts, n_seq * n_exp * CAP, 2 * width)
-    routed_up, routed_down = got[:, :, :width], got[:, :, width:]
-
-    pre_act = jnp.einsum("erd,edh->erh", routed_up, w_in, preferred_element_type=F32)
-    activation = jax.nn.silu(pre_act).astype(BF16)
-    expert_out = jnp.einsum("erh,ehd->erd", activation, w_out, preferred_element_type=F32).astype(BF16)
-    act_grad = jnp.einsum("erd,ehd->erh", routed_down, w_out, preferred_element_type=F32)
-    pre_grad = (act_grad * silu_slope(pre_act)).astype(BF16)
-    input_grad = jnp.einsum("erh,edh->erd", pre_grad, w_in, preferred_element_type=F32).astype(BF16)
-    back = jnp.concatenate([expert_out, input_grad], axis=2)
-    back = back.reshape(experts, n_seq, n_exp, CAP, 2 * width).transpose(1, 2, 0, 3, 4)
-    back = back.reshape(n_seq, n_exp * per_dest, 2 * width)
-    back = lax.psum_scatter(back, "seq", scatter_dimension=0, tiled=False)
-    back = back.reshape(n_exp, per_dest, 2 * width)
-    back = lax.all_to_all(back, "exp", split_axis=0, concat_axis=0, tiled=True)
+    back, routed, activation, pre_grad = run_experts(both, w_in, w_out)
+    routed_up, routed_down = routed[:, :, :width], routed[:, :, width:]
     back = back.reshape(slots, 2 * width)
 
     w_out_grad = jnp.einsum("erh,erd->ehd", activation, routed_down, preferred_element_type=F32)

time: 198 us -> 132 us (0.67)
  waiting for transfers between devices: 94.2 us -> 0.01 us
  Pallas kernels: 0 us -> 88.2 us
  blocking collectives: 30.2 us -> 0 us
  between operations: 14.3 us -> 0.84 us
  local copies, waits for them, and re-layouts: 13.9 us -> 5.37 us
  starting transfers between devices: 17.9 us -> 10.9 us
  matrix products: 20 us -> 16.7 us
  other arithmetic: 7.18 us -> 9.38 us
    pallas_call x0 -> x1, Pallas kernels: none -> 88.2 us  [run_experts(): pl.pallas_call(functools.partial(expert_kernel, n_seq, n_exp), out_shape=...]
    reduce_scatter x1 -> x0, waiting for transfers between devices: 44.3 us -> none  [per_device(): back = lax.psum_scatter(back, 'seq', scatter_dimension=0, tiled=False)]
    all_gather x1 -> x0, waiting for transfers between devices: 34.2 us -> none  [per_device(): got = lax.all_gather(got, 'seq', axis=0, tiled=False)]
    all_to_all x1 -> x0, blocking collectives: 30.2 us -> none  [per_device(): got = lax.all_to_all(both, 'exp', split_axis=0, concat_axis=0, tiled=True)]
    all_to_all x1 -> x0, waiting for transfers between devices: 13.4 us -> none  [per_device(): back = lax.all_to_all(back, 'exp', split_axis=0, concat_axis=0, tiled=True)]
    dot_general x4 -> x0, matrix products: 5.5 us -> none  [the longest x1 1.68 us: per_device(): jnp.einsum('erd,ehd->erh', routed_down, w_out, preferred_element_type=F32)]
    reshape x2 -> x0, local copies, waits for them, and re-layouts: 5.25 us -> none  [the longest x1 2.65 us: per_device(): got = got.reshape(experts, n_seq * n_exp * CAP, 2 * width)]
    all_to_all x1 -> x0, starting transfers between devices: 5.23 us -> none  [per_device(): back = lax.all_to_all(back, 'exp', split_axis=0, concat_axis=0, tiled=True)]
  transfers between devices with their start and end apart: 7 -> 4, of which waited for: 4 -> 0; matrix products, arithmetic and copies ran while one was open for 9% -> 15% of each run, Pallas kernels for 0% -> 0%
where the time goes in v2:
time: 132 us; the launch traced here: 131 us
  Pallas kernels  88.2 us (67%)
  matrix products  16.7 us (13%)
  starting transfers between devices  10.9 us (8%)
  other arithmetic  9.38 us (7%)
  local copies, waits for them, and re-layouts  5.37 us (4%)
    pallas_call x1, Pallas kernels, run_experts(): pl.pallas_call(functools.partial(expert_kernel, n_seq, n_exp), out_shape=...  88.2 us
    dot_general x1, matrix products, per_device(): jnp.einsum('erd,erh->edh', routed_up, pre_grad, preferred_element_type=F32)  6.46 us
    ppermute x2, starting transfers between devices, edge_rows(): low = lax.ppermute(block[-width:], 'seq', forward)  6.46 us
    dot_general x1, matrix products, per_device(): jnp.einsum('erh,erd->ehd', activation, routed_down, preferred_element_typ...  4.73 us
    ppermute x2, starting transfers between devices, edge_rows(): high = lax.ppermute(block[:width], 'seq', backward)  4.48 us
    convert_element_type x1, other arithmetic, per_device(): hidden = (frames[0].astype(F32) + jax.nn.silu(mixing)).astype(BF16)  3.13 us
    broadcast_in_dim x1, other arithmetic, per_device(): return (mixed.astype(BF16)[None], frames_grad[None], w_in_grad, w_out_grad)  2.76 us
  transfers between devices with their start and end apart: 4, of which 0 were waited for; matrix products, arithmetic and copies ran while one was open for 15% of the time, Pallas kernels for 0%

profile of v2, /device:TPU:1, one launch (start us, length us, event | category | flops | bytes accessed | tf_op | source)
XLA Modules:
  0.0 131.4 jit_solution(2433035035808760216)
XLA Ops:
  0.6 0.8 slice_bitcast_fusion.1
  1.4 4.5 %collective-permute-start = (bf16[15,1024]{1,0:T(8,128)(2,1)S(1)}, bf16[15,1024]{1,0:T(8,128)(2,1)S(1)}, u32[]{:S(2)}, u32[]{:S(2)}) collective-permute-start(bf16[15,1024]{1,0:T(8,128)(2,1)S(1)} %get-tuple-element.18), channel_id=1, source_target_pairs={{0,8},{8,16},{16,24},{1,9},{9,17},{17,25},{2,10},{10,18},{18,26},{... | collective-permute-start | bytes 92168 | tf_op jit(solution)/shard_map/ppermute | solution.py:26
  6.0 1.9 %collective-permute-start.1 = (bf16[15,1024]{1,0:T(8,128)(2,1)S(1)}, bf16[15,1024]{1,0:T(8,128)(2,1)S(1)}, u32[]{:S(2)}, u32[]{:S(2)}) collective-permute-start(bf16[15,1024]{1,0:T(8,128)(2,1)S(1)} %get-tuple-element.19), channel_id=1, source_target_pairs={{8,0},{16,8},{24,16},{9,1},{17,9},{25,17},{10,2},{18,10},{26,18},{... | collective-permute-start | bytes 92168 | tf_op jit(solution)/shard_map/ppermute | solution.py:27
  7.9 0.8 slice_bitcast_fusion.2
  8.7 0.8 copy.21
  9.5 0.1 eq.64
  9.6 0.2 convert_reduce_fusion
  9.8 0.1 reduce_sum.30
  10.0 0.2 slice_reduce_fusion
  10.1 1.4 %fusion.98 = (f32[1,1024]{1,0:T(1,128)S(1)}, f32[1,1024]{1,0:T(1,128)S(1)}, f32[1,1024]{1,0:T(1,128)S(1)}, f32[1,1024]{1,0:T(1,128)S(1)}, f32[1,1024]{1,0:T(1,12...) fusion(f32[31,1024]{1,0:T(8,128)} %param.8), kind=kLoop, calls=%fused_computation.192 | loop fusion | bytes 155648 | tf_op jit(solution)/shard_map/slice | solution.py:36
  11.6 0.8 fusion.77
  12.3 0.1 select_reduce_fusion
  12.5 1.4 %fusion.4 = bf16[256,1024]{1,0:T(8,128)(2,1)S(1)} fusion(f32[256]{0:T(256)S(1)} %add.297, bf16[1,128,1024]{2,1,0:T(8,128)(2,1)} %param.13, s32[128]{0:T(128)S(1)} %get-tuple-element.12, s32[128]{0:T(128)S(1)} %get-tuple-element.13), kind=kOutput, calls=%fused_computation.5 | convolution fusion | flops 67731456 | bytes 788480 | tf_op jit(solution)/shard_map/ts,td->sd/dot_general | solution.py:359
  13.8 1.1 fusion.99
  15.0 0.0 collective-permute-done
  15.0 0.0 collective-permute-done.1
  15.0 1.0 maximum_convert_fusion
  16.0 3.1 %add_convert_fusion = (bf16[128,1024]{1,0:T(8,128)(2,1)S(1)}, f32[128,1024]{1,0:T(8,128)S(1)}) fusion(bf16[1,128,1024]{2,1,0:T(8,128)(2,1)} %param.7, f32[158,1024]{1,0:T(8,128)S(1)} %maximum_convert_fusion, f32[1024]{0:T(1024)S(1)} %bitcast.120, f32[1024]{0:T(1024)S(1)} %bitcast.122, f32[1024]{0:T(1024)S(1)} %bitcast.64, f32[1024]{0:T(1024)S(1)} %bitcast.66, ...), kind=kLoop, calls=%fused_computation.141 | loop fusion | flops 8912896 | bytes 17428480 | tf_op jit(solution)/shard_map/convert_element_type | solution.py:356
  19.2 0.4 convolution_convert_fusion
  19.6 1.1 pad_maximum_fusion
  20.7 88.2 %expert_exchange.1 = (bf16[8,32,2048]{2,1,0:T(8,128)(2,1)}, bf16[4,256,2048]{2,1,0:T(8,128)(2,1)}, bf16[4,256,512]{2,1,0:T(8,128)(2,1)}, bf16[4,256,512]{2,1,0:T(8,128)(2,1)}) custom-call(bf16[8,32,2048]{2,1,0:T(8,128)(2,1)} %bitcast.57, bf16[256,256]{1,0:T(8,128)(2,1)} %get-tuple-element.52.sort_ref, bf16[256,256]{1,0:T(8,128)(2,1)} %get-tuple-element.51.unsort_ref, ...), custom_call_target="tpu_custom_call" | custom-call | tf_op jit(solution)/shard_map/expert_exchange/pallas_call | solution.py:305
  108.8 0.0 copy-start.3
  108.9 1.4 %fusion.6 = f32[128,1024]{1,0:T(8,128)S(1)} fusion(bf16[128,1024]{1,0:T(8,128)(2,1)S(1)} %get-tuple-element.14, bf16[256,2048]{1,0:T(8,128)(2,1)} %bitcast.58, f32[128]{0:T(128)S(1)} %get-tuple-element.54, s32[128]{0:T(128)S(1)} %get-tuple-element.13), kind=kOutput, calls=%fused_computation.11 | convolution fusion | flops 67534848 | bytes 1311744 | tf_op jit(solution)/shard_map/dot_general | solution.py:373
  110.3 1.4 %convolution_add_fusion = f32[128,1024]{1,0:T(8,128)S(1)} fusion(bf16[256,2048]{1,0:T(8,128)(2,1)} %bitcast.59, bf16[1,128,1024]{2,1,0:T(8,128)(2,1)} %param.13, s32[128]{0:T(128)S(1)} %get-tuple-element.12, s32[128]{0:T(128)S(1)} %get-tuple-element.13), kind=kOutput, calls=%fused_computation.7 | convolution fusion | flops 67469312 | bytes 1311744 | tf_op jit(solution)/shard_map/dot_general | solution.py:375
  111.7 0.2 multiply_convert_fusion
  111.9 1.9 %collective-permute-start.2 = (bf16[15,1024]{1,0:T(8,128)(2,1)S(1)}, bf16[15,1024]{1,0:T(8,128)(2,1)S(1)}, u32[]{:S(2)}, u32[]{:S(2)}) collective-permute-start(bf16[15,1024]{1,0:T(8,128)(2,1)S(1)} %get-tuple-element.16), channel_id=1, source_target_pairs={{0,8},{8,16},{16,24},{1,9},{9,17},{17,25},{2,10},{10,18},{18,26},{... | collective-permute-start | bytes 92168 | tf_op jit(solution)/shard_map/ppermute | solution.py:26
  113.8 2.6 %collective-permute-start.3 = (bf16[15,1024]{1,0:T(8,128)(2,1)S(1)}, bf16[15,1024]{1,0:T(8,128)(2,1)S(1)}, u32[]{:S(2)}, u32[]{:S(2)}) collective-permute-start(bf16[15,1024]{1,0:T(8,128)(2,1)S(1)} %get-tuple-element.17), channel_id=1, source_target_pairs={{8,0},{16,8},{24,16},{9,1},{17,9},{25,17},{10,2},{18,10},{26,18},{... | collective-permute-start | bytes 92168 | tf_op jit(solution)/shard_map/ppermute | solution.py:27
  116.4 0.0 copy-done.3
  116.4 0.0 copy-start
  116.4 0.0 copy-start.1
  116.4 6.5 %fusion.2 = f32[4,1024,512]{2,1,0:T(8,128)} fusion(bf16[4,256,512]{2,1,0:T(8,128)(2,1)S(1)} %copy-done.3, bf16[4,256,2048]{2,1,0:T(8,128)(2,1)} %get-tuple-element.9), kind=kOutput, calls=%fused_computation.2 | convolution fusion | flops 1073741824 | bytes 11534336 | tf_op jit(solution)/shard_map/erd,erh->edh/dot_general | solution.py:369
  122.9 0.0 copy-done
  122.9 0.0 copy-done.1
  122.9 0.0 copy-start.2
  122.9 4.7 %fusion = f32[4,512,1024]{2,1,0:T(8,128)} fusion(bf16[4,256,512]{2,1,0:T(8,128)(2,1)S(1)} %copy-done.1, bf16[4,256,2048]{2,1,0:T(8,128)(2,1)S(1)} %copy-done), kind=kOutput, calls=%fused_computation | convolution fusion | flops 1073741824 | bytes 11534336 | tf_op jit(solution)/shard_map/erh,erd->ehd/dot_general | solution.py:368
  127.6 0.0 copy-done.2
  127.6 1.0 fusion.8
  128.6 0.0 collective-permute-done.2
  128.6 0.0 collective-permute-done.3
  128.6 0.1 maximum_convert_fusion.1
  128.7 2.8 %fusion.78 = bf16[1,128,1024]{2,1,0:T(8,128)(2,1)} fusion(f32[128,1024]{1,0:T(8,128)S(1)} %convolution_add_fusion, f32[158,1024]{1,0:T(8,128)S(1)} %maximum_convert_fusion.1, f32[1024]{0:T(1024)S(1)} %bitcast.121, f32[1024]{0:T(1024)S(1)} %bitcast.123, f32[1024]{0:T(1024)S(1)} %bitcast.65, f32[1024]{0:T(1024)S(1)} %bitcast.67, f32[1024]{0:T(1024)S(1)} %bitcast.69, ...), kind=kLoop, calls=%fused_computation.155 | loop fusion | flops 8257536 | bytes 17166336 | tf_op jit(solution)/shard_map/broadcast_in_dim | solution.py:379
  (4 shorter events, 0.0 us)
Async XLA Ops:
  1.4 13.6 %collective-permute-start = (bf16[15,1024]{1,0:T(8,128)(2,1)S(1)}, bf16[15,1024]{1,0:T(8,128)(2,1)S(1)}, u32[]{:S(2)}, u32[]{:S(2)}) collective-permute-start(bf16[15,1024]{1,0:T(8,128)(2,1)S(1)} %get-tuple-element.18), channel_id=1, source_target_pairs={{0,8},{8,16},{16,24},{1,9},{9,17},{17,25},{2,10},{10,18},{18,26},{... | collective-permute-start | bytes 92168 | tf_op jit(solution)/shard_map/ppermute | solution.py:26
  6.0 9.0 %collective-permute-start.1 = (bf16[15,1024]{1,0:T(8,128)(2,1)S(1)}, bf16[15,1024]{1,0:T(8,128)(2,1)S(1)}, u32[]{:S(2)}, u32[]{:S(2)}) collective-permute-start(bf16[15,1024]{1,0:T(8,128)(2,1)S(1)} %get-tuple-element.19), channel_id=1, source_target_pairs={{8,0},{16,8},{24,16},{9,1},{17,9},{25,17},{10,2},{18,10},{26,18},{... | collective-permute-start | bytes 92168 | tf_op jit(solution)/shard_map/ppermute | solution.py:27
  108.8 7.5 %copy-start.3 = (bf16[4,256,512]{2,1,0:T(8,128)(2,1)S(1)}, bf16[4,256,512]{2,1,0:T(8,128)(2,1)}, u32[]{:S(2)}) copy-start(bf16[4,256,512]{2,1,0:T(8,128)(2,1)} %get-tuple-element.10) | copy-start | bytes 3145732
  111.9 16.7 %collective-permute-start.2 = (bf16[15,1024]{1,0:T(8,128)(2,1)S(1)}, bf16[15,1024]{1,0:T(8,128)(2,1)S(1)}, u32[]{:S(2)}, u32[]{:S(2)}) collective-permute-start(bf16[15,1024]{1,0:T(8,128)(2,1)S(1)} %get-tuple-element.16), channel_id=1, source_target_pairs={{0,8},{8,16},{16,24},{1,9},{9,17},{17,25},{2,10},{10,18},{18,26},{... | collective-permute-start | bytes 92168 | tf_op jit(solution)/shard_map/ppermute | solution.py:26
  113.8 14.8 %collective-permute-start.3 = (bf16[15,1024]{1,0:T(8,128)(2,1)S(1)}, bf16[15,1024]{1,0:T(8,128)(2,1)S(1)}, u32[]{:S(2)}, u32[]{:S(2)}) collective-permute-start(bf16[15,1024]{1,0:T(8,128)(2,1)S(1)} %get-tuple-element.17), channel_id=1, source_target_pairs={{8,0},{16,8},{24,16},{9,1},{17,9},{25,17},{10,2},{18,10},{26,18},{... | collective-permute-start | bytes 92168 | tf_op jit(solution)/shard_map/ppermute | solution.py:27
  116.4 6.5 %copy-start = (bf16[4,256,2048]{2,1,0:T(8,128)(2,1)S(1)}, bf16[4,256,2048]{2,1,0:T(8,128)(2,1)}, u32[]{:S(2)}) copy-start(bf16[4,256,2048]{2,1,0:T(8,128)(2,1)} %get-tuple-element.9) | copy-start | bytes 12582916
  116.4 6.5 %copy-start.1 = (bf16[4,256,512]{2,1,0:T(8,128)(2,1)S(1)}, bf16[4,256,512]{2,1,0:T(8,128)(2,1)}, u32[]{:S(2)}) copy-start(bf16[4,256,512]{2,1,0:T(8,128)(2,1)} %get-tuple-element.11) | copy-start | bytes 3145732
  122.9 4.7 %copy-start.2 = (bf16[8,32,2048]{2,1,0:T(8,128)(2,1)S(1)}, bf16[8,32,2048]{2,1,0:T(8,128)(2,1)}, u32[]{:S(2)}) copy-start(bf16[8,32,2048]{2,1,0:T(8,128)(2,1)} %get-tuple-element.8) | copy-start | bytes 3145732

commit v3 on v2

--- a/solution.py
+++ b/solution.py
@@ -67,6 +67,13 @@
             device_id=(s, e), device_id_type=MESH,
         )
 
+    def other(k):
+        total, bit = 0, 1
+        while bit < n_exp:
+            total = total + lax.rem(me_e // bit + k // bit, 2) * bit
+            bit *= 2
+        return total
+
     def same_core(y):
         return lax.rem(y, n_y) * 2 + me_c
 
@@ -84,11 +91,11 @@
     for j in range(1, n_y):
         greet(same_core(me_y + j), me_e)
     for k in range(1, n_exp):
-        greet(me_s, lax.rem(me_e + k, n_exp))
+        greet(me_s, other(k))
     pl.semaphore_wait(barrier, 1 + n_y - 1 + n_exp - 1)
 
     def exp_copy(k):
-        target = lax.rem(me_e + k, n_exp)
+        target = other(k)
         return remote(
             send_ref.at[target], part(me_s, k), exp_send.at[k], exp_recv.at[k], me_s, target
         )
@@ -110,7 +117,9 @@
 
         lax.fori_loop(low, high, step, 0)
 
-    loop(1, n_exp, lambda k: exp_copy(k).start())
+    half = n_exp // 2
+    for k in [1, half, half + 1, *range(2, half)]:
+        exp_copy(k).start()
     part(me_s, 0)[...] = send_ref[me_e]
 
     def pass_on(k):
@@ -131,13 +140,17 @@
         exp_copy(k).wait_recv()
         pass_on(k)
 
-        @pl.when(k >= 2)
+        @pl.when((k >= half) & (k < n_exp - 2))
         def _():
-            pass_far(k - 2)
+            exp_copy(k).wait_send()
+            exp_copy(k + 2).start()
+
+        @pl.when(k >= half)
+        def _():
+            pass_far(k - half)
 
     loop(1, n_exp, arrive)
-    pass_far(n_exp - 2)
-    pass_far(n_exp - 1)
+    loop(half, n_exp, pass_far)
 
     def settle(k):
         for j in range(n_y):
@@ -146,7 +159,8 @@
             y_copy(j, k).wait_send()
 
     loop(0, n_exp, settle)
-    loop(1, n_exp, lambda k: exp_copy(k).wait_send())
+    for k in [*range(1, half), n_exp - 2, n_exp - 1]:
+        exp_copy(k).wait_send()
 
     small = group_rows // experts
     columns = 512
@@ -231,18 +245,10 @@
     def home_copy(k):
         return remote(
             part(me_s, k), back_ref.at[me_e], back_send.at[k], back_recv.at[k],
-            me_s, lax.rem(me_e + n_exp - k, n_exp),
-        )
-
-    def order(i):
-        return lax.rem(i + 1, n_exp)
-
-    def pair_start(i):
-        for j in [*range(1, n_y), 0]:
-            pair_copy(j, order(i)).start()
-
-    def y_stage(i):
-        k = order(i)
+            me_s, other(k),
+        )
+
+    def y_stage(k):
         for j in range(1, n_y):
             pair_copy(j, k).wait_recv()
             y = lax.rem(me_y + j, n_y)
@@ -258,30 +264,44 @@
             summed = summed + y_got[j - 1, k].astype(F32)
         return summed.astype(BF16)
 
-    loop(0, n_exp, pair_start)
-    loop(0, n_exp, y_stage)
-
     def home_stage(k):
-        part(me_s, k)[...] = total(k)
-        home_copy(k).start()
-
-    loop(1, n_exp, home_stage)
-    back_ref[me_e] = total(0)
+        if k == 0:
+            back_ref[me_e] = total(0)
+        else:
+            part(me_s, k)[...] = total(k)
+            home_copy(k).start()
+
+    def y_sent(k):
+        for j in range(1, n_y):
+            y_sum_copy(j, k).wait_send()
+
+    order = [*range(half, n_exp), *range(1, half), 0]
+    for k in order:
+        for j in range(1, n_y):
+            pair_copy(j, k).start()
+    for k in order:
+        pair_copy(0, k).start()
+    for i, k in enumerate(order):
+        if i >= 2:
+            y_sent(order[i - 2])
+        y_stage(k)
+        if i >= 2:
+            home_stage(order[i - 2])
+    for k in order[-2:]:
+        home_stage(k)
+        y_sent(k)
 
     def finish(k):
         for j in range(n_y):
             pair_copy(j, k).wait_send()
-        for j in range(1, n_y):
-            y_sum_copy(j, k).wait_send()
 
     loop(0, n_exp, finish)
 
     def come_home(k):
         home_copy(k).wait_send()
-        pltpu.make_async_remote_copy(
-            src_ref=part(me_s, k), dst_ref=back_ref.at[lax.rem(me_e + k, n_exp)],
-            send_sem=back_send.at[k], recv_sem=back_recv.at[k],
-            device_id=(me_s, lax.rem(me_e + n_exp - k, n_exp)), device_id_type=MESH,
+        remote(
+            part(me_s, k), back_ref.at[other(k)], back_send.at[k], back_recv.at[k],
+            me_s, other(k),
         ).wait_recv()
 
     loop(1, n_exp, come_home)

time: 132 us -> 119 us (0.902)
  Pallas kernels: 88.2 us -> 73.7 us
  starting transfers between devices: 10.9 us -> 12.6 us
    pallas_call x1, Pallas kernels: 88.2 us -> 73.7 us  [run_experts(): pl.pallas_call(functools.partial(expert_kernel, n_seq, n_exp), out_shape=...]
    ppermute x2, starting transfers between devices: 6.46 us -> 8.79 us  [edge_rows(): low = lax.ppermute(block[-width:], 'seq', forward)]
  transfers between devices with their start and end apart: 4 -> 4, of which waited for: 0 -> 0; matrix products, arithmetic and copies ran while one was open for 15% -> 16% of each run, Pallas kernels for 0% -> 0%
where the time goes in v3:
time: 119 us
  Pallas kernels  73.7 us (62%)
  matrix products  16.7 us (14%)
  starting transfers between devices  12.6 us (11%)
  other arithmetic  9.38 us (8%)
  local copies, waits for them, and re-layouts  5.37 us (5%)
    pallas_call x1, Pallas kernels, run_experts(): pl.pallas_call(functools.partial(expert_kernel, n_seq, n_exp), out_shape=...  73.7 us
    ppermute x2, starting transfers between devices, edge_rows(): low = lax.ppermute(block[-width:], 'seq', forward)  8.79 us
    dot_general x1, matrix products, per_device(): jnp.einsum('erd,erh->edh', routed_up, pre_grad, preferred_element_type=F32)  6.46 us
    dot_general x1, matrix products, per_device(): jnp.einsum('erh,erd->ehd', activation, routed_down, preferred_element_typ...  4.73 us
    ppermute x2, starting transfers between devices, edge_rows(): high = lax.ppermute(block[:width], 'seq', backward)  3.84 us
    convert_element_type x1, other arithmetic, per_device(): hidden = (frames[0].astype(F32) + jax.nn.silu(mixing)).astype(BF16)  3.13 us
    broadcast_in_dim x1, other arithmetic, per_device(): return (mixed.astype(BF16)[None], frames_grad[None], w_in_grad, w_out_grad)  2.76 us
    slice x2, local copies, waits for them, and re-layouts, local_conv(): summed = summed + kernel[tap_index] * padded[offset:offset + length]  2.55 us
  transfers between devices with their start and end apart: 4, of which 0 were waited for; matrix products, arithmetic and copies ran while one was open for 16% of the time, Pallas kernels for 0%

profile of v3, /device:TPU:1, one launch (start us, length us, event | category | flops | bytes accessed | tf_op | source)
XLA Modules:
  0.0 118.6 jit_solution(14486644340586161898)
XLA Ops:
  0.6 0.8 slice_bitcast_fusion.1
  1.4 4.5 %collective-permute-start = (bf16[15,1024]{1,0:T(8,128)(2,1)S(1)}, bf16[15,1024]{1,0:T(8,128)(2,1)S(1)}, u32[]{:S(2)}, u32[]{:S(2)}) collective-permute-start(bf16[15,1024]{1,0:T(8,128)(2,1)S(1)} %get-tuple-element.18), channel_id=1, source_target_pairs={{0,8},{8,16},{16,24},{1,9},{9,17},{17,25},{2,10},{10,18},{18,26},{... | collective-permute-start | bytes 92168 | tf_op jit(solution)/shard_map/ppermute | solution.py:26
  6.0 1.9 %collective-permute-start.1 = (bf16[15,1024]{1,0:T(8,128)(2,1)S(1)}, bf16[15,1024]{1,0:T(8,128)(2,1)S(1)}, u32[]{:S(2)}, u32[]{:S(2)}) collective-permute-start(bf16[15,1024]{1,0:T(8,128)(2,1)S(1)} %get-tuple-element.19), channel_id=1, source_target_pairs={{8,0},{16,8},{24,16},{9,1},{17,9},{25,17},{10,2},{18,10},{26,18},{... | collective-permute-start | bytes 92168 | tf_op jit(solution)/shard_map/ppermute | solution.py:27
  7.9 0.8 slice_bitcast_fusion.2
  8.7 0.8 copy.21
  9.5 0.1 eq.64
  9.6 0.2 convert_reduce_fusion
  9.8 0.1 reduce_sum.30
  10.0 0.2 slice_reduce_fusion
  10.1 1.4 %fusion.98 = (f32[1,1024]{1,0:T(1,128)S(1)}, f32[1,1024]{1,0:T(1,128)S(1)}, f32[1,1024]{1,0:T(1,128)S(1)}, f32[1,1024]{1,0:T(1,128)S(1)}, f32[1,1024]{1,0:T(1,12...) fusion(f32[31,1024]{1,0:T(8,128)} %param.8), kind=kLoop, calls=%fused_computation.192 | loop fusion | bytes 155648 | tf_op jit(solution)/shard_map/slice | solution.py:36
  11.6 0.8 fusion.77
  12.3 0.1 select_reduce_fusion
  12.5 1.4 %fusion.4 = bf16[256,1024]{1,0:T(8,128)(2,1)S(1)} fusion(f32[256]{0:T(256)S(1)} %add.297, bf16[1,128,1024]{2,1,0:T(8,128)(2,1)} %param.13, s32[128]{0:T(128)S(1)} %get-tuple-element.12, s32[128]{0:T(128)S(1)} %get-tuple-element.13), kind=kOutput, calls=%fused_computation.5 | convolution fusion | flops 67731456 | bytes 788480 | tf_op jit(solution)/shard_map/ts,td->sd/dot_general | solution.py:379
  13.8 1.1 fusion.99
  15.0 0.0 collective-permute-done
  15.0 0.0 collective-permute-done.1
  15.0 1.0 maximum_convert_fusion
  16.0 3.1 %add_convert_fusion = (bf16[128,1024]{1,0:T(8,128)(2,1)S(1)}, f32[128,1024]{1,0:T(8,128)S(1)}) fusion(bf16[1,128,1024]{2,1,0:T(8,128)(2,1)} %param.7, f32[158,1024]{1,0:T(8,128)S(1)} %maximum_convert_fusion, f32[1024]{0:T(1024)S(1)} %bitcast.120, f32[1024]{0:T(1024)S(1)} %bitcast.122, f32[1024]{0:T(1024)S(1)} %bitcast.64, f32[1024]{0:T(1024)S(1)} %bitcast.66, ...), kind=kLoop, calls=%fused_computation.141 | loop fusion | flops 8912896 | bytes 17428480 | tf_op jit(solution)/shard_map/convert_element_type | solution.py:376
  19.2 0.4 convolution_convert_fusion
  19.6 1.1 pad_maximum_fusion
  20.7 73.7 %expert_exchange.1 = (bf16[8,32,2048]{2,1,0:T(8,128)(2,1)}, bf16[4,256,2048]{2,1,0:T(8,128)(2,1)}, bf16[4,256,512]{2,1,0:T(8,128)(2,1)}, bf16[4,256,512]{2,1,0:T(8,128)(2,1)}) custom-call(bf16[8,32,2048]{2,1,0:T(8,128)(2,1)} %bitcast.57, bf16[256,256]{1,0:T(8,128)(2,1)} %get-tuple-element.52.sort_ref, bf16[256,256]{1,0:T(8,128)(2,1)} %get-tuple-element.51.unsort_ref, ...), custom_call_target="tpu_custom_call" | custom-call | tf_op jit(solution)/shard_map/expert_exchange/pallas_call | solution.py:325
  94.4 0.0 copy-start.3
  94.4 1.4 %fusion.6 = f32[128,1024]{1,0:T(8,128)S(1)} fusion(bf16[128,1024]{1,0:T(8,128)(2,1)S(1)} %get-tuple-element.14, bf16[256,2048]{1,0:T(8,128)(2,1)} %bitcast.58, f32[128]{0:T(128)S(1)} %get-tuple-element.54, s32[128]{0:T(128)S(1)} %get-tuple-element.13), kind=kOutput, calls=%fused_computation.11 | convolution fusion | flops 67534848 | bytes 1311744 | tf_op jit(solution)/shard_map/dot_general | solution.py:393
  95.8 1.4 %convolution_add_fusion = f32[128,1024]{1,0:T(8,128)S(1)} fusion(bf16[256,2048]{1,0:T(8,128)(2,1)} %bitcast.59, bf16[1,128,1024]{2,1,0:T(8,128)(2,1)} %param.13, s32[128]{0:T(128)S(1)} %get-tuple-element.12, s32[128]{0:T(128)S(1)} %get-tuple-element.13), kind=kOutput, calls=%fused_computation.7 | convolution fusion | flops 67469312 | bytes 1311744 | tf_op jit(solution)/shard_map/dot_general | solution.py:395
  97.2 0.2 multiply_convert_fusion
  97.4 4.2 %collective-permute-start.2 = (bf16[15,1024]{1,0:T(8,128)(2,1)S(1)}, bf16[15,1024]{1,0:T(8,128)(2,1)S(1)}, u32[]{:S(2)}, u32[]{:S(2)}) collective-permute-start(bf16[15,1024]{1,0:T(8,128)(2,1)S(1)} %get-tuple-element.16), channel_id=1, source_target_pairs={{0,8},{8,16},{16,24},{1,9},{9,17},{17,25},{2,10},{10,18},{18,26},{... | collective-permute-start | bytes 92168 | tf_op jit(solution)/shard_map/ppermute | solution.py:26
  101.6 1.9 %collective-permute-start.3 = (bf16[15,1024]{1,0:T(8,128)(2,1)S(1)}, bf16[15,1024]{1,0:T(8,128)(2,1)S(1)}, u32[]{:S(2)}, u32[]{:S(2)}) collective-permute-start(bf16[15,1024]{1,0:T(8,128)(2,1)S(1)} %get-tuple-element.17), channel_id=1, source_target_pairs={{8,0},{16,8},{24,16},{9,1},{17,9},{25,17},{10,2},{18,10},{26,18},{... | collective-permute-start | bytes 92168 | tf_op jit(solution)/shard_map/ppermute | solution.py:27
  103.6 0.0 copy-done.3
  103.6 0.0 copy-start
  103.6 0.0 copy-start.1
  103.6 6.5 %fusion.2 = f32[4,1024,512]{2,1,0:T(8,128)} fusion(bf16[4,256,512]{2,1,0:T(8,128)(2,1)S(1)} %copy-done.3, bf16[4,256,2048]{2,1,0:T(8,128)(2,1)} %get-tuple-element.9), kind=kOutput, calls=%fused_computation.2 | convolution fusion | flops 1073741824 | bytes 11534336 | tf_op jit(solution)/shard_map/erd,erh->edh/dot_general | solution.py:389
  110.1 0.0 copy-done
  110.1 0.0 copy-done.1
  110.1 0.0 copy-start.2
  110.1 4.7 %fusion = f32[4,512,1024]{2,1,0:T(8,128)} fusion(bf16[4,256,512]{2,1,0:T(8,128)(2,1)S(1)} %copy-done.1, bf16[4,256,2048]{2,1,0:T(8,128)(2,1)S(1)} %copy-done), kind=kOutput, calls=%fused_computation | convolution fusion | flops 1073741824 | bytes 11534336 | tf_op jit(solution)/shard_map/erh,erd->ehd/dot_general | solution.py:388
  114.8 0.0 copy-done.2
  114.8 1.0 fusion.8
  115.8 0.0 collective-permute-done.2
  115.8 0.0 collective-permute-done.3
  115.8 0.1 maximum_convert_fusion.1
  115.9 2.8 %fusion.78 = bf16[1,128,1024]{2,1,0:T(8,128)(2,1)} fusion(f32[128,1024]{1,0:T(8,128)S(1)} %convolution_add_fusion, f32[158,1024]{1,0:T(8,128)S(1)} %maximum_convert_fusion.1, f32[1024]{0:T(1024)S(1)} %bitcast.121, f32[1024]{0:T(1024)S(1)} %bitcast.123, f32[1024]{0:T(1024)S(1)} %bitcast.65, f32[1024]{0:T(1024)S(1)} %bitcast.67, f32[1024]{0:T(1024)S(1)} %bitcast.69, ...), kind=kLoop, calls=%fused_computation.155 | loop fusion | flops 8257536 | bytes 17166336 | tf_op jit(solution)/shard_map/broadcast_in_dim | solution.py:399
  (4 shorter events, 0.0 us)
Async XLA Ops:
  1.4 13.6 %collective-permute-start = (bf16[15,1024]{1,0:T(8,128)(2,1)S(1)}, bf16[15,1024]{1,0:T(8,128)(2,1)S(1)}, u32[]{:S(2)}, u32[]{:S(2)}) collective-permute-start(bf16[15,1024]{1,0:T(8,128)(2,1)S(1)} %get-tuple-element.18), channel_id=1, source_target_pairs={{0,8},{8,16},{16,24},{1,9},{9,17},{17,25},{2,10},{10,18},{18,26},{... | collective-permute-start | bytes 92168 | tf_op jit(solution)/shard_map/ppermute | solution.py:26
  6.0 9.0 %collective-permute-start.1 = (bf16[15,1024]{1,0:T(8,128)(2,1)S(1)}, bf16[15,1024]{1,0:T(8,128)(2,1)S(1)}, u32[]{:S(2)}, u32[]{:S(2)}) collective-permute-start(bf16[15,1024]{1,0:T(8,128)(2,1)S(1)} %get-tuple-element.19), channel_id=1, source_target_pairs={{8,0},{16,8},{24,16},{9,1},{17,9},{25,17},{10,2},{18,10},{26,18},{... | collective-permute-start | bytes 92168 | tf_op jit(solution)/shard_map/ppermute | solution.py:27
  94.4 9.2 %copy-start.3 = (bf16[4,256,512]{2,1,0:T(8,128)(2,1)S(1)}, bf16[4,256,512]{2,1,0:T(8,128)(2,1)}, u32[]{:S(2)}) copy-start(bf16[4,256,512]{2,1,0:T(8,128)(2,1)} %get-tuple-element.10) | copy-start | bytes 3145732
  97.4 18.4 %collective-permute-start.2 = (bf16[15,1024]{1,0:T(8,128)(2,1)S(1)}, bf16[15,1024]{1,0:T(8,128)(2,1)S(1)}, u32[]{:S(2)}, u32[]{:S(2)}) collective-permute-start(bf16[15,1024]{1,0:T(8,128)(2,1)S(1)} %get-tuple-element.16), channel_id=1, source_target_pairs={{0,8},{8,16},{16,24},{1,9},{9,17},{17,25},{2,10},{10,18},{18,26},{... | collective-permute-start | bytes 92168 | tf_op jit(solution)/shard_map/ppermute | solution.py:26
  101.6 14.1 %collective-permute-start.3 = (bf16[15,1024]{1,0:T(8,128)(2,1)S(1)}, bf16[15,1024]{1,0:T(8,128)(2,1)S(1)}, u32[]{:S(2)}, u32[]{:S(2)}) collective-permute-start(bf16[15,1024]{1,0:T(8,128)(2,1)S(1)} %get-tuple-element.17), channel_id=1, source_target_pairs={{8,0},{16,8},{24,16},{9,1},{17,9},{25,17},{10,2},{18,10},{26,18},{... | collective-permute-start | bytes 92168 | tf_op jit(solution)/shard_map/ppermute | solution.py:27
  103.6 6.5 %copy-start = (bf16[4,256,2048]{2,1,0:T(8,128)(2,1)S(1)}, bf16[4,256,2048]{2,1,0:T(8,128)(2,1)}, u32[]{:S(2)}) copy-start(bf16[4,256,2048]{2,1,0:T(8,128)(2,1)} %get-tuple-element.9) | copy-start | bytes 12582916
  103.6 6.5 %copy-start.1 = (bf16[4,256,512]{2,1,0:T(8,128)(2,1)S(1)}, bf16[4,256,512]{2,1,0:T(8,128)(2,1)}, u32[]{:S(2)}) copy-start(bf16[4,256,512]{2,1,0:T(8,128)(2,1)} %get-tuple-element.11) | copy-start | bytes 3145732
  110.1 4.7 %copy-start.2 = (bf16[8,32,2048]{2,1,0:T(8,128)(2,1)S(1)}, bf16[8,32,2048]{2,1,0:T(8,128)(2,1)}, u32[]{:S(2)}) copy-start(bf16[8,32,2048]{2,1,0:T(8,128)(2,1)} %get-tuple-element.8) | copy-start | bytes 3145732
